TPU v7x, 32 devices: a whole 2x2x4 slice. The times are simulated.
32 devices in a mesh: dp: 8 (over z, x), tensor: 4 (over y, core).
Axes of the slice: x: 2, y: 2, z: 4, core: 2. Of those that a mesh axis runs over, the one named last changes fastest.
Arguments:
- tokens: bfloat16 [2048, 768], P('dp'), may hold values from -6 to 6
- cotangent: bfloat16 [2048, 768], P('dp'), may hold values from -6 to 6
- segment_ids: int32 [8, 256], P('dp'), may hold values from 0 to 2, never falling along the last dimension, each value on 1 to 160 neighbouring positions
- routes: int32 [2048, 2], P('dp'), may hold values from 0 to 3, all different within a row; in each aligned block of 256 rows (0 to 255, 256 to 511, ...) at most 144 rows name the same one
- buckets: int32 [256], replicated, may hold values from 0 to 31, as said below
- gain_attn: bfloat16 [768], P('dp'), may hold values from 0.5 to 1.5
- w_query: bfloat16 [768, 768], P('dp', 'tensor'), may hold values from -0.21875 to 0.21875
- w_key: bfloat16 [768, 768], P('dp', 'tensor'), may hold values from -0.21875 to 0.21875
- w_value: bfloat16 [768, 768], P('dp', 'tensor'), may hold values from -0.21875 to 0.21875
- w_out_t: bfloat16 [768, 768], P('dp', 'tensor'), may hold values from -1.25 to 1.25
- gain_moe: bfloat16 [768], P('dp'), may hold values from 0.5 to 1.5
- w_router: bfloat16 [768, 4], P('dp'), may hold values from -0.15625 to 0.15625
- w_gate: bfloat16 [4, 768, 3072], P(None, 'dp', 'tensor'), may hold values from -0.21875 to 0.21875
- w_up: bfloat16 [4, 768, 3072], P(None, 'dp', 'tensor'), may hold values from -0.21875 to 0.21875
- w_down_t: bfloat16 [4, 768, 3072], P(None, 'dp', 'tensor'), may hold values from -0.3125 to 0.3125
- bias_table: bfloat16 [12, 32], P('tensor'), may hold values from -4 to 4
Outputs:
- output: bfloat16 [2048, 768], P('dp')
- grad_tokens: bfloat16 [2048, 768], P('dp')
- grad_gain_attn: float32 [768], P('dp')
- grad_w_query: float32 [768, 768], P('dp', 'tensor')
- grad_w_key: float32 [768, 768], P('dp', 'tensor')
- grad_w_value: float32 [768, 768], P('dp', 'tensor')
- grad_w_out_t: float32 [768, 768], P('dp', 'tensor')
- grad_gain_moe: float32 [768], P('dp')
- grad_w_router: float32 [768, 4], P('dp')
- grad_w_gate: float32 [4, 768, 3072], P(None, 'dp', 'tensor')
- grad_w_up: float32 [4, 768, 3072], P(None, 'dp', 'tensor')
- grad_w_down_t: float32 [4, 768, 3072], P(None, 'dp', 'tensor')
- grad_bias_table: float32 [12, 32], P('tensor')
Inputs may be any that keep to these rules, and one draw needn't show every extreme that they name: `routes`: in each sequence no expert is named by more than 144 tokens, a bound that some block reaches; a token's experts differ. `segment_ids`: never falling along a sequence. `buckets`: 0 at distance 0, never falling with the distance, 31 at distance 256 - 1.
All inputs are finite; a program needn't handle non-finite values.
Results may differ from a plain program's by a relative error of at most 0.017.
Values may be sent and summed in bfloat16 or wider, within the bound.
A program may use at most 192 MiB of HBM per device.

v0:
```python
import jax
import jax.numpy as jnp
from jax import lax
from jax.sharding import PartitionSpec as P

DH = 64
CAP = 144


EPSILON = 1e-06
NEG_FILL = -1e30
HIGHEST = lax.Precision.HIGHEST


def rms_scale(values, gain_vec):
    inverse = lax.rsqrt(jnp.mean(values * values, axis=-1, keepdims=True) + EPSILON)
    return values * inverse * gain_vec


def gated_unit(gate_act, up_act):
    return jax.nn.gelu(gate_act, approximate=False) * up_act


def soft_router(logits):
    return jax.nn.softmax(logits, axis=-1)


def slot_tables(routes, n_experts, capacity):
    seq_len = routes.shape[0]
    position = jnp.arange(seq_len, dtype=jnp.int32)
    expert_ids = jnp.arange(n_experts, dtype=jnp.int32)
    pick_hot = (routes[:, :, None] == expert_ids[None, None, :]).astype(jnp.int32)
    chosen = jnp.sum(pick_hot, axis=1)
    slot_place = jnp.cumsum(chosen, axis=0) - 1
    pick_slot = jnp.sum(pick_hot * slot_place[:, None, :], axis=2)
    flat_slot = routes * capacity + pick_slot
    slot_ids = jnp.arange(capacity, dtype=jnp.int32)
    slot_match = (
        (slot_place[None, :, :] == slot_ids[:, None, None]) & (chosen[None, :, :] == 1)
    ).astype(jnp.int32)
    slot_row = jnp.sum(slot_match * position[None, :, None], axis=1)
    slot_live = jnp.sum(slot_match, axis=1).astype(jnp.float32)
    return (pick_hot, flat_slot, slot_row, slot_live)


def block_scores(query_blk, key_all, dist_bias, seg_blk, segment, start_row, qk_scale):
    block_rows = query_blk.shape[0]
    seq_len = key_all.shape[0]
    raw_scores = (
        jnp.einsum("qhd,khd->hqk", query_blk, key_all, preferred_element_type=jnp.float32)
        * qk_scale
    )
    row_pos = start_row + jnp.arange(block_rows, dtype=jnp.int32)
    col_pos = jnp.arange(seq_len, dtype=jnp.int32)
    offset = row_pos[:, None] - col_pos[None, :]
    allowed = (offset >= 0) & (seg_blk[:, None] == segment[None, :])
    bias_blk = jnp.take(dist_bias, jnp.clip(offset, 0, seq_len - 1), axis=1)
    return jnp.where(allowed[None, :, :], raw_scores + bias_blk, NEG_FILL)


def diagonal_sums(d_scores, start_row):
    n_heads, block_rows, seq_len = d_scores.shape
    reverse = d_scores[:, :, ::-1]
    padded = jnp.pad(reverse, ((0, 0), (0, 0), (0, block_rows)))
    flat_view = padded.reshape(n_heads, block_rows * (seq_len + block_rows))[
        :, : block_rows * (seq_len + block_rows - 1)
    ]
    skewed = flat_view.reshape(n_heads, block_rows, seq_len + block_rows - 1)
    column_sums = jnp.sum(skewed, axis=1)
    extended = jnp.pad(column_sums, ((0, 0), (0, seq_len + 1 - block_rows)))
    return lax.dynamic_slice_in_dim(extended, seq_len - 1 - start_row, seq_len, 1)


def attention_forward(queries, key_all, values, dist_bias, segment, qk_scale, block_rows):
    seq_len, n_heads, head_dim = queries.shape

    def one_block(block_index):
        start_row = block_index * block_rows
        scores = block_scores(queries, key_all, dist_bias, segment, segment, start_row, qk_scale)
        row_max = jnp.max(scores, axis=-1, keepdims=True)
        exp_scores = jnp.exp(scores - row_max)
        row_total = jnp.sum(exp_scores, axis=-1, keepdims=True)
        prob_bf = (exp_scores / row_total).astype(jnp.bfloat16)
        mixed_blk = jnp.einsum("hqk,khd->qhd", prob_bf, values, preferred_element_type=jnp.float32)
        return (mixed_blk.astype(jnp.bfloat16), (row_max + jnp.log(row_total))[:, :, 0])

    mixed_all, log_total = lax.map(one_block, jnp.arange(seq_len // block_rows, dtype=jnp.int32))
    mixed_out = mixed_all.reshape(seq_len, n_heads * head_dim)
    log_total = jnp.transpose(log_total, (1, 0, 2)).reshape(n_heads, seq_len)
    return (mixed_out, log_total)


def attention_backward(
    queries, key_all, values, d_mixed, log_total, dist_bias, segment, qk_scale, block_rows
):
    seq_len, n_heads, head_dim = queries.shape

    def one_block(running, block_index):
        d_keys, d_values, d_dist = running
        start_row = block_index * block_rows
        scores = block_scores(queries, key_all, dist_bias, segment, segment, start_row, qk_scale)
        prob_full = jnp.exp(scores - log_total[:, :, None])
        d_prob = jnp.einsum("qhd,khd->hqk", d_mixed, values, preferred_element_type=jnp.float32)
        row_dot = jnp.sum(prob_full * d_prob, axis=-1, keepdims=True)
        d_scores = prob_full * (d_prob - row_dot)
        d_scores_bf = d_scores.astype(jnp.bfloat16)
        d_query_blk = (
            jnp.einsum("hqk,khd->qhd", d_scores_bf, key_all, preferred_element_type=jnp.float32)
            * qk_scale
        )
        d_keys = (
            d_keys
            + jnp.einsum("hqk,qhd->khd", d_scores_bf, queries, preferred_element_type=jnp.float32)
            * qk_scale
        )
        d_values = d_values + jnp.einsum(
            "hqk,qhd->khd",
            prob_full.astype(jnp.bfloat16),
            d_mixed,
            preferred_element_type=jnp.float32,
        )
        d_dist = d_dist + diagonal_sums(d_scores, start_row)
        return ((d_keys, d_values, d_dist), d_query_blk)

    zeros_kv = jnp.zeros((seq_len, n_heads, head_dim), jnp.float32)
    start_carry = (zeros_kv, zeros_kv, jnp.zeros((n_heads, seq_len), jnp.float32))
    (d_keys, d_values, d_dist), d_query_all = lax.scan(
        one_block, start_carry, jnp.arange(seq_len // block_rows, dtype=jnp.int32)
    )
    columns = n_heads * head_dim
    return (
        d_query_all.reshape(seq_len, columns),
        d_keys.reshape(seq_len, columns),
        d_values.reshape(seq_len, columns),
        d_dist,
    )


def body(
    tokens,
    cotangent,
    segment_ids,
    routes,
    buckets,
    gain_attn,
    w_query,
    w_key,
    w_value,
    w_out_t,
    gain_moe,
    w_router,
    w_gate,
    w_up,
    w_down_t,
    bias_table,
):
    seq_len, model_width = tokens.shape
    n_picks = routes.shape[1]
    n_experts = w_gate.shape[0]
    n_heads = bias_table.shape[0]
    n_buckets = bias_table.shape[1]
    qk_scale = DH ** (-0.5)
    block_rows = min(512, seq_len)
    segment = segment_ids[0]
    attn_set = (
        lax.all_gather(gain_attn, "dp", axis=0, tiled=True),
        lax.all_gather(w_query, "dp", axis=0, tiled=True),
        lax.all_gather(w_key, "dp", axis=0, tiled=True),
        lax.all_gather(w_value, "dp", axis=0, tiled=True),
        lax.all_gather(w_out_t, "dp", axis=0, tiled=True),
        lax.all_gather(gain_moe, "dp", axis=0, tiled=True),
        lax.all_gather(w_router, "dp", axis=0, tiled=True),
    )
    attn_gain, query_full, key_full, value_full, out_full, moe_gain, router_full = attn_set
    token_f = tokens.astype(jnp.float32)
    attn_gain_f = attn_gain.astype(jnp.float32)
    normed = rms_scale(token_f, attn_gain_f).astype(jnp.bfloat16)
    queries = (
        jnp.dot(normed, query_full, preferred_element_type=jnp.float32)
        .astype(jnp.bfloat16)
        .reshape(seq_len, n_heads, DH)
    )
    key_all = (
        jnp.dot(normed, key_full, preferred_element_type=jnp.float32)
        .astype(jnp.bfloat16)
        .reshape(seq_len, n_heads, DH)
    )
    values = (
        jnp.dot(normed, value_full, preferred_element_type=jnp.float32)
        .astype(jnp.bfloat16)
        .reshape(seq_len, n_heads, DH)
    )
    dist_hot = (buckets[:, None] == jnp.arange(n_buckets, dtype=jnp.int32)[None, :]).astype(
        jnp.float32
    )
    dist_bias = jnp.dot(bias_table.astype(jnp.float32), dist_hot.T, precision=HIGHEST)
    mixed_out, log_total = attention_forward(
        queries, key_all, values, dist_bias, segment, qk_scale, block_rows
    )
    attn_part = jnp.dot(mixed_out, out_full.T, preferred_element_type=jnp.float32)
    attn_out = lax.psum(attn_part, "tensor")
    residual = token_f + attn_out
    moe_gain_f = moe_gain.astype(jnp.float32)
    normed_moe = rms_scale(residual, moe_gain_f).astype(jnp.bfloat16)
    logits = jnp.dot(normed_moe, router_full, preferred_element_type=jnp.float32)
    router = soft_router(logits)
    pick_hot, flat_slot, slot_row, slot_live = slot_tables(routes, n_experts, CAP)
    pick_float = pick_hot.astype(jnp.float32)
    kept_weights = []
    kept_acts = []
    outputs = []
    for expert in range(n_experts):
        expert_set = (
            lax.all_gather(w_gate[expert], "dp", axis=0, tiled=True),
            lax.all_gather(w_up[expert], "dp", axis=0, tiled=True),
            lax.all_gather(w_down_t[expert], "dp", axis=0, tiled=True),
        )
        expert_rows = jnp.take(normed_moe, slot_row[:, expert], axis=0)
        gate_act = jnp.dot(expert_rows, expert_set[0], preferred_element_type=jnp.float32)
        up_act = jnp.dot(expert_rows, expert_set[1], preferred_element_type=jnp.float32)
        inner_act = gated_unit(gate_act, up_act).astype(jnp.bfloat16)
        outputs.append(jnp.dot(inner_act, expert_set[2].T, preferred_element_type=jnp.float32))
        kept_weights.append(expert_set)
        kept_acts.append((expert_rows, gate_act, up_act, inner_act))
    stacked = jnp.concatenate(outputs, axis=0)
    picked = jnp.take(stacked, flat_slot.reshape(-1), axis=0).reshape(seq_len, n_picks, model_width)
    gates = jnp.sum(router[:, None, :] * pick_float, axis=2)
    moe_part = jnp.sum(gates[:, :, None] * picked, axis=1)
    moe_out = lax.psum(moe_part.astype(jnp.bfloat16), "tensor").astype(jnp.float32)
    output = (residual + moe_out).astype(jnp.bfloat16)
    grad_final = cotangent.astype(jnp.float32)
    gate_dots = jnp.sum(picked * grad_final[:, None, :], axis=2)
    d_router_part = jnp.sum(gate_dots[:, :, None] * pick_float, axis=1)
    d_router = lax.psum(d_router_part, "tensor")
    gate_slot = jnp.take_along_axis(router, slot_row, axis=0) * slot_live
    grad_rows = []
    gate_shares = []
    up_shares = []
    down_shares = []
    for expert in range(n_experts):
        expert_set = (
            lax.all_gather(w_gate[expert], "dp", axis=0, tiled=True),
            lax.all_gather(w_up[expert], "dp", axis=0, tiled=True),
            lax.all_gather(w_down_t[expert], "dp", axis=0, tiled=True),
        )
        expert_rows, gate_act, up_act, inner_act = kept_acts[expert]
        d_out = (
            gate_slot[:, expert : expert + 1] * jnp.take(grad_final, slot_row[:, expert], axis=0)
        ).astype(jnp.bfloat16)
        d_inner = jnp.dot(d_out, expert_set[2], preferred_element_type=jnp.float32)
        unused, unit_pull = jax.vjp(gated_unit, gate_act, up_act)
        d_gate_act, d_up_act = unit_pull(d_inner)
        d_gate_bf = d_gate_act.astype(jnp.bfloat16)
        d_up_bf = d_up_act.astype(jnp.bfloat16)
        grad_down = jnp.dot(d_out.T, inner_act, preferred_element_type=jnp.float32)
        grad_gate = jnp.dot(expert_rows.T, d_gate_bf, preferred_element_type=jnp.float32)
        grad_up = jnp.dot(expert_rows.T, d_up_bf, preferred_element_type=jnp.float32)
        grad_rows.append(
            jnp.dot(d_gate_bf, expert_set[0].T, preferred_element_type=jnp.float32)
            + jnp.dot(d_up_bf, expert_set[1].T, preferred_element_type=jnp.float32)
        )
        gate_share, up_share, down_share = (
            lax.psum_scatter(grad_gate, "dp", scatter_dimension=0, tiled=True),
            lax.psum_scatter(grad_up, "dp", scatter_dimension=0, tiled=True),
            lax.psum_scatter(grad_down, "dp", scatter_dimension=0, tiled=True),
        )
        gate_shares.append(gate_share)
        up_shares.append(up_share)
        down_shares.append(down_share)
    grad_stack = jnp.concatenate(grad_rows, axis=0)
    d_moe_part = jnp.sum(
        jnp.take(grad_stack, flat_slot.reshape(-1), axis=0).reshape(seq_len, n_picks, model_width),
        axis=1,
    )
    d_moe = lax.psum(d_moe_part, "tensor")
    back_set = (
        lax.all_gather(gain_attn, "dp", axis=0, tiled=True),
        lax.all_gather(w_query, "dp", axis=0, tiled=True),
        lax.all_gather(w_key, "dp", axis=0, tiled=True),
        lax.all_gather(w_value, "dp", axis=0, tiled=True),
        lax.all_gather(w_out_t, "dp", axis=0, tiled=True),
        lax.all_gather(gain_moe, "dp", axis=0, tiled=True),
        lax.all_gather(w_router, "dp", axis=0, tiled=True),
    )
    back_attn_gain, back_query, back_key, back_value, back_out, back_moe_gain, back_router = (
        back_set
    )
    unused, soft_pull = jax.vjp(soft_router, logits)
    d_logits_bf = soft_pull(d_router)[0].astype(jnp.bfloat16)
    grad_router = jnp.dot(normed_moe.T, d_logits_bf, preferred_element_type=jnp.float32)
    d_normed_moe = d_moe + jnp.dot(d_logits_bf, back_router.T, preferred_element_type=jnp.float32)
    unused, moe_pull = jax.vjp(rms_scale, residual, back_moe_gain.astype(jnp.float32))
    d_resid_norm, grad_moe_gain = moe_pull(d_normed_moe)
    d_residual = grad_final + d_resid_norm
    d_branch = d_residual.astype(jnp.bfloat16)
    grad_out = jnp.dot(d_branch.T, mixed_out, preferred_element_type=jnp.float32)
    d_mixed = (
        jnp.dot(d_branch, back_out, preferred_element_type=jnp.float32)
        .astype(jnp.bfloat16)
        .reshape(seq_len, n_heads, DH)
    )
    d_queries, d_keys, d_values, d_dist = attention_backward(
        queries, key_all, values, d_mixed, log_total, dist_bias, segment, qk_scale, block_rows
    )
    d_queries_bf = d_queries.astype(jnp.bfloat16)
    d_keys_bf = d_keys.astype(jnp.bfloat16)
    d_values_bf = d_values.astype(jnp.bfloat16)
    grad_table = jnp.dot(d_dist, dist_hot, precision=HIGHEST)
    grad_query = jnp.dot(normed.T, d_queries_bf, preferred_element_type=jnp.float32)
    grad_key = jnp.dot(normed.T, d_keys_bf, preferred_element_type=jnp.float32)
    grad_value = jnp.dot(normed.T, d_values_bf, preferred_element_type=jnp.float32)
    d_normed_part = jnp.dot(d_queries_bf, back_query.T, preferred_element_type=jnp.float32)
    d_normed_part = d_normed_part + jnp.dot(
        d_keys_bf, back_key.T, preferred_element_type=jnp.float32
    )
    d_normed_part = d_normed_part + jnp.dot(
        d_values_bf, back_value.T, preferred_element_type=jnp.float32
    )
    d_normed = lax.psum(d_normed_part.astype(jnp.bfloat16), "tensor").astype(jnp.float32)
    unused, first_pull = jax.vjp(rms_scale, token_f, back_attn_gain.astype(jnp.float32))
    d_token_norm, grad_attn_gain = first_pull(d_normed)
    grad_tokens = (d_residual + d_token_norm).astype(jnp.bfloat16)
    gate_total = jnp.stack(gate_shares, axis=0)
    up_total = jnp.stack(up_shares, axis=0)
    down_total = jnp.stack(down_shares, axis=0)
    shares = (
        lax.psum_scatter(grad_attn_gain, "dp", scatter_dimension=0, tiled=True),
        lax.psum_scatter(grad_query, "dp", scatter_dimension=0, tiled=True),
        lax.psum_scatter(grad_key, "dp", scatter_dimension=0, tiled=True),
        lax.psum_scatter(grad_value, "dp", scatter_dimension=0, tiled=True),
        lax.psum_scatter(grad_out, "dp", scatter_dimension=0, tiled=True),
        lax.psum_scatter(grad_moe_gain, "dp", scatter_dimension=0, tiled=True),
        lax.psum_scatter(grad_router, "dp", scatter_dimension=0, tiled=True),
    )
    table_total = lax.psum(grad_table, "dp")
    return (
        output,
        grad_tokens,
        shares[0],
        shares[1],
        shares[2],
        shares[3],
        shares[4],
        shares[5],
        shares[6],
        gate_total,
        up_total,
        down_total,
        table_total,
    )


def solution(mesh):
    in_specs = (
        P("dp", None),
        P("dp", None),
        P("dp", None),
        P("dp", None),
        P(),
        P("dp"),
        P("dp", "tensor"),
        P("dp", "tensor"),
        P("dp", "tensor"),
        P("dp", "tensor"),
        P("dp"),
        P("dp", None),
        P(None, "dp", "tensor"),
        P(None, "dp", "tensor"),
        P(None, "dp", "tensor"),
        P("tensor", None),
    )
    out_specs = (
        P("dp", None),
        P("dp", None),
        P("dp"),
        P("dp", "tensor"),
        P("dp", "tensor"),
        P("dp", "tensor"),
        P("dp", "tensor"),
        P("dp"),
        P("dp", None),
        P(None, "dp", "tensor"),
        P(None, "dp", "tensor"),
        P(None, "dp", "tensor"),
        P("tensor", None),
    )
    return jax.shard_map(body, mesh=mesh, in_specs=in_specs, out_specs=out_specs, check_vma=False)
```

profile of v0, /device:TPU:0, one launch (start us, length us, event | category | flops | bytes accessed | tf_op | source)
XLA Modules:
  0.0 2137.6 jit_solution(6977159407559317367)
XLA Ops:
  8.2 33.0 %all_gather.77 = bf16[768,192]{1,0:T(8,128)(2,1)S(1)} all-gather(bf16[96,192]{1,0:T(8,128)(2,1)} %param.32), channel_id=1, replica_groups=mesh['dp'=8,'tensor'=4] {'dp'}, dimensions={0}, use_global_device_ids=true | all-gather | bytes 331776 | tf_op jit(solution)/shard_map/all_gather | solution.py:169
  68.1 217.1 %gather_fusion.1 = f32[65536,3]{1,0:T(8,128)} fusion(f32[3,256]{0,1:T(8,128)S(1)} %copy.81, s32[65536]{0:T(1024)S(1)} %broadcast_clamp_fusion), kind=kCustom, calls=%fused_computation.clone | custom fusion | bytes 1835008 | tf_op jit(solution)/shard_map/while/body/eval_jaxpr/jit(_take)/gather | solution.py:57
  304.4 31.1 %all_gather.78 = bf16[768,192]{1,0:T(8,128)(2,1)S(1)} all-gather(bf16[96,192]{1,0:T(8,128)(2,1)S(1)} %copy-done.81), channel_id=1, replica_groups=mesh['dp'=8,'tensor'=4] {'dp'}, dimensions={0}, use_global_device_ids=true | all-gather | bytes 331776 | tf_op jit(solution)/shard_map/all_gather | solution.py:167
  336.4 31.2 %all_gather.79 = bf16[768,192]{1,0:T(8,128)(2,1)S(1)} all-gather(bf16[96,192]{1,0:T(8,128)(2,1)S(1)} %copy-done.82), channel_id=1, replica_groups=mesh['dp'=8,'tensor'=4] {'dp'}, dimensions={0}, use_global_device_ids=true | all-gather | bytes 331776 | tf_op jit(solution)/shard_map/all_gather | solution.py:168
  368.3 31.0 %all_gather.80 = bf16[768,192]{1,0:T(8,128)(2,1)S(1)} all-gather(bf16[96,192]{1,0:T(8,128)(2,1)S(1)} %copy-done.83), channel_id=1, replica_groups=mesh['dp'=8,'tensor'=4] {'dp'}, dimensions={0}, use_global_device_ids=true | all-gather | bytes 331776 | tf_op jit(solution)/shard_map/all_gather | solution.py:170
  455.2 31.0 %all-gather.48.cloned.1.call-done = bf16[1,768,768]{2,1,0:T(8,128)(2,1)} async-done(((bf16[1,96,768]{2,1,0:T(8,128)(2,1)}), bf16[1,768,768]{2,1,0:T(8,128)(2,1)}) %all-gather.48.cloned.1.call-update) | async-done | bytes 1179664 | tf_op jit(solution)/shard_map/all_gather | solution.py:216
  489.8 38.5 %all-gather.46.cloned.1.call-done = bf16[1,768,768]{2,1,0:T(8,128)(2,1)} async-done(((bf16[1,96,768]{2,1,0:T(8,128)(2,1)}), bf16[1,768,768]{2,1,0:T(8,128)(2,1)}) %all-gather.46.cloned.1.call-update) | async-done | bytes 1179664 | tf_op jit(solution)/shard_map/all_gather | solution.py:215
  532.5 38.0 %all-gather.38.cloned.1.call-done = bf16[1,768,768]{2,1,0:T(8,128)(2,1)} async-done(((bf16[1,96,768]{2,1,0:T(8,128)(2,1)}), bf16[1,768,768]{2,1,0:T(8,128)(2,1)}) %all-gather.38.cloned.1.call-update) | async-done | bytes 1179664 | tf_op jit(solution)/shard_map/all_gather | solution.py:214
  572.9 39.8 %all-gather.42.cloned.1.call-done = bf16[1,768,768]{2,1,0:T(8,128)(2,1)} async-done(((bf16[1,96,768]{2,1,0:T(8,128)(2,1)}), bf16[1,768,768]{2,1,0:T(8,128)(2,1)}) %all-gather.42.cloned.1.call-update) | async-done | bytes 1179664 | tf_op jit(solution)/shard_map/all_gather | solution.py:216
  616.4 38.6 %all-gather.40.cloned.1.call-done = bf16[1,768,768]{2,1,0:T(8,128)(2,1)} async-done(((bf16[1,96,768]{2,1,0:T(8,128)(2,1)}), bf16[1,768,768]{2,1,0:T(8,128)(2,1)}) %all-gather.40.cloned.1.call-update) | async-done | bytes 1179664 | tf_op jit(solution)/shard_map/all_gather | solution.py:215
  659.2 37.9 %all-gather.32.cloned.1.call-done = bf16[1,768,768]{2,1,0:T(8,128)(2,1)} async-done(((bf16[1,96,768]{2,1,0:T(8,128)(2,1)}), bf16[1,768,768]{2,1,0:T(8,128)(2,1)}) %all-gather.32.cloned.1.call-update) | async-done | bytes 1179664 | tf_op jit(solution)/shard_map/all_gather | solution.py:214
  699.5 39.7 %all-gather.36.cloned.1.call-done = bf16[1,768,768]{2,1,0:T(8,128)(2,1)} async-done(((bf16[1,96,768]{2,1,0:T(8,128)(2,1)}), bf16[1,768,768]{2,1,0:T(8,128)(2,1)}) %all-gather.36.cloned.1.call-update) | async-done | bytes 1179664 | tf_op jit(solution)/shard_map/all_gather | solution.py:216
  742.7 38.6 %all-gather.34.cloned.1.call-done = bf16[1,768,768]{2,1,0:T(8,128)(2,1)} async-done(((bf16[1,96,768]{2,1,0:T(8,128)(2,1)}), bf16[1,768,768]{2,1,0:T(8,128)(2,1)}) %all-gather.34.cloned.1.call-update) | async-done | bytes 1179664 | tf_op jit(solution)/shard_map/all_gather | solution.py:215
  785.5 38.6 %all-gather.26.cloned.1.call-done = bf16[1,768,768]{2,1,0:T(8,128)(2,1)} async-done(((bf16[1,96,768]{2,1,0:T(8,128)(2,1)}), bf16[1,768,768]{2,1,0:T(8,128)(2,1)}) %all-gather.26.cloned.1.call-update) | async-done | bytes 1179664 | tf_op jit(solution)/shard_map/all_gather | solution.py:214
  825.8 40.4 %all-gather.30.cloned.1.call-done = bf16[1,768,768]{2,1,0:T(8,128)(2,1)} async-done(((bf16[1,96,768]{2,1,0:T(8,128)(2,1)}), bf16[1,768,768]{2,1,0:T(8,128)(2,1)}) %all-gather.30.cloned.1.call-update) | async-done | bytes 1179664 | tf_op jit(solution)/shard_map/all_gather | solution.py:216
  869.4 39.0 %all-gather.28.cloned.1.call-done = bf16[1,768,768]{2,1,0:T(8,128)(2,1)} async-done(((bf16[1,96,768]{2,1,0:T(8,128)(2,1)}), bf16[1,768,768]{2,1,0:T(8,128)(2,1)}) %all-gather.28.cloned.1.call-update) | async-done | bytes 1179664 | tf_op jit(solution)/shard_map/all_gather | solution.py:215
  1034.3 37.5 %all-reduce.5 = (f32[768]{0:T(1024)S(1)}, f32[768]{0:T(1024)S(1)}, f32[3,32]{1,0:T(4,128)}) all-reduce(f32[768]{0:T(1024)S(1)} %get-tuple-element.67, f32[768]{0:T(1024)S(1)} %copy-done.93, f32[3,32]{1,0:T(4,128)S(1)} %fusion.102), channel_id=14, replica_groups=mesh['dp'=8,'tensor'=4] {'dp'}, use_global_device_ids=true, to_apply=%region_27.32.clone | all-reduce | flops 1632 | bytes 13056
  1082.1 71.5 %reduce-scatter.32.cloned.1.call-done = f32[96,768]{1,0:T(8,128)} async-done(((f32[768,768]{1,0:T(8,128)}), f32[96,768]{1,0:T(8,128)}) %reduce-scatter.32.cloned.1.call-update) | async-done | bytes 294928 | tf_op jit(solution)/shard_map/reduce_scatter | solution.py:263
  1153.6 71.5 %reduce-scatter.30.cloned.1.call-done = f32[96,768]{1,0:T(8,128)} async-done(((f32[768,768]{1,0:T(8,128)}), f32[96,768]{1,0:T(8,128)}) %reduce-scatter.30.cloned.1.call-update) | async-done | bytes 294928 | tf_op jit(solution)/shard_map/reduce_scatter | solution.py:263
  1225.1 71.5 %reduce-scatter.28.cloned.1.call-done = f32[96,768]{1,0:T(8,128)} async-done(((f32[768,768]{1,0:T(8,128)}), f32[96,768]{1,0:T(8,128)}) %reduce-scatter.28.cloned.1.call-update) | async-done | bytes 294928 | tf_op jit(solution)/shard_map/reduce_scatter | solution.py:263
  1298.9 69.2 %reduce-scatter.42.cloned.1.call-done = f32[96,768]{1,0:T(8,128)} async-done(((f32[768,768]{1,0:T(8,128)}), f32[96,768]{1,0:T(8,128)}) %reduce-scatter.42.cloned.1.call-update) | async-done | bytes 294928 | tf_op jit(solution)/shard_map/reduce_scatter | solution.py:264
  1368.1 71.2 %reduce-scatter.40.cloned.1.call-done = f32[96,768]{1,0:T(8,128)} async-done(((f32[768,768]{1,0:T(8,128)}), f32[96,768]{1,0:T(8,128)}) %reduce-scatter.40.cloned.1.call-update) | async-done | bytes 294928 | tf_op jit(solution)/shard_map/reduce_scatter | solution.py:264
  1439.3 71.4 %reduce-scatter.38.cloned.1.call-done = f32[96,768]{1,0:T(8,128)} async-done(((f32[768,768]{1,0:T(8,128)}), f32[96,768]{1,0:T(8,128)}) %reduce-scatter.38.cloned.1.call-update) | async-done | bytes 294928 | tf_op jit(solution)/shard_map/reduce_scatter | solution.py:264
  1510.7 71.4 %reduce-scatter.36.cloned.1.call-done = f32[96,768]{1,0:T(8,128)} async-done(((f32[768,768]{1,0:T(8,128)}), f32[96,768]{1,0:T(8,128)}) %reduce-scatter.36.cloned.1.call-update) | async-done | bytes 294928 | tf_op jit(solution)/shard_map/reduce_scatter | solution.py:264
  1584.4 69.0 %reduce-scatter.50.cloned.1.call-done = f32[96,768]{1,0:T(8,128)} async-done(((f32[768,768]{1,0:T(8,128)}), f32[96,768]{1,0:T(8,128)}) %reduce-scatter.50.cloned.1.call-update) | async-done | bytes 294928 | tf_op jit(solution)/shard_map/reduce_scatter | solution.py:265
  1653.5 71.3 %reduce-scatter.48.cloned.1.call-done = f32[96,768]{1,0:T(8,128)} async-done(((f32[768,768]{1,0:T(8,128)}), f32[96,768]{1,0:T(8,128)}) %reduce-scatter.48.cloned.1.call-update) | async-done | bytes 294928 | tf_op jit(solution)/shard_map/reduce_scatter | solution.py:265
  1724.8 71.5 %reduce-scatter.46.cloned.1.call-done = f32[96,768]{1,0:T(8,128)} async-done(((f32[768,768]{1,0:T(8,128)}), f32[96,768]{1,0:T(8,128)}) %reduce-scatter.46.cloned.1.call-update) | async-done | bytes 294928 | tf_op jit(solution)/shard_map/reduce_scatter | solution.py:265
  1796.3 71.4 %reduce-scatter.44.cloned.1.call-done = f32[96,768]{1,0:T(8,128)} async-done(((f32[768,768]{1,0:T(8,128)}), f32[96,768]{1,0:T(8,128)}) %reduce-scatter.44.cloned.1.call-update) | async-done | bytes 294928 | tf_op jit(solution)/shard_map/reduce_scatter | solution.py:265
  1870.0 63.1 %reduce-scatter.20.cloned.1.call-done = f32[96,192]{1,0:T(8,128)} async-done(((f32[768,192]{1,0:T(8,128)}), f32[96,192]{1,0:T(8,128)}) %reduce-scatter.20.cloned.1.call-update) | async-done | bytes 73744 | tf_op jit(solution)/shard_map/reduce_scatter | solution.py:328
  1933.2 65.8 %reduce-scatter.22.cloned.1.call-done = f32[96,192]{1,0:T(8,128)} async-done(((f32[768,192]{1,0:T(8,128)}), f32[96,192]{1,0:T(8,128)}) %reduce-scatter.22.cloned.1.call-update) | async-done | bytes 73744 | tf_op jit(solution)/shard_map/reduce_scatter | solution.py:329
  1999.0 65.3 %reduce-scatter.24.cloned.1.call-done = f32[96,192]{1,0:T(8,128)} async-done(((f32[768,192]{1,0:T(8,128)}), f32[96,192]{1,0:T(8,128)}) %reduce-scatter.24.cloned.1.call-update) | async-done | bytes 73744 | tf_op jit(solution)/shard_map/reduce_scatter | solution.py:330
  2064.3 65.7 %reduce-scatter.26.cloned.1.call-done = f32[96,192]{1,0:T(8,128)} async-done(((f32[768,192]{1,0:T(8,128)}), f32[96,192]{1,0:T(8,128)}) %reduce-scatter.26.cloned.1.call-update) | async-done | bytes 73744 | tf_op jit(solution)/shard_map/reduce_scatter | solution.py:331
  (486 shorter events, 277.0 us)
Async XLA Ops:
  8.0 433.4 %all-reduce.12.cloned.1.call-start = ((), (), s32[]{:S(2)}) async-start(), calls=%async_computation.17 | async-start | bytes 1572864 | tf_op jit(solution)/shard_map/psum | solution.py:201
  402.0 50.7 %all-gather.44.cloned.1.call-start = ((), (), s32[]{:S(2)}) async-start(), calls=%async_computation.44 | async-start | bytes 1327104 | tf_op jit(solution)/shard_map/all_gather | solution.py:214
  402.9 83.3 %all-gather.48.cloned.1.call-start = ((), (), s32[]{:S(2)}) async-start(), calls=%async_computation.46 | async-start | bytes 1327104 | tf_op jit(solution)/shard_map/all_gather | solution.py:216
  404.0 124.2 %all-gather.46.cloned.1.call-start = ((), (), s32[]{:S(2)}) async-start(), calls=%async_computation.45 | async-start | bytes 1327104 | tf_op jit(solution)/shard_map/all_gather | solution.py:215
  405.0 165.5 %all-gather.38.cloned.1.call-start = ((), (), s32[]{:S(2)}) async-start(), calls=%async_computation.41 | async-start | bytes 1327104 | tf_op jit(solution)/shard_map/all_gather | solution.py:214
  405.7 207.0 %all-gather.42.cloned.1.call-start = ((), (), s32[]{:S(2)}) async-start(), calls=%async_computation.43 | async-start | bytes 1327104 | tf_op jit(solution)/shard_map/all_gather | solution.py:216
  406.5 248.5 %all-gather.40.cloned.1.call-start = ((), (), s32[]{:S(2)}) async-start(), calls=%async_computation.42 | async-start | bytes 1327104 | tf_op jit(solution)/shard_map/all_gather | solution.py:215
  407.2 289.9 %all-gather.32.cloned.1.call-start = ((), (), s32[]{:S(2)}) async-start(), calls=%async_computation.38 | async-start | bytes 1327104 | tf_op jit(solution)/shard_map/all_gather | solution.py:214
  407.8 331.4 %all-gather.36.cloned.1.call-start = ((), (), s32[]{:S(2)}) async-start(), calls=%async_computation.40 | async-start | bytes 1327104 | tf_op jit(solution)/shard_map/all_gather | solution.py:216
  408.4 372.9 %all-gather.34.cloned.1.call-start = ((), (), s32[]{:S(2)}) async-start(), calls=%async_computation.39 | async-start | bytes 1327104 | tf_op jit(solution)/shard_map/all_gather | solution.py:215
  409.0 415.1 %all-gather.26.cloned.1.call-start = ((), (), s32[]{:S(2)}) async-start(), calls=%async_computation.35 | async-start | bytes 1327104 | tf_op jit(solution)/shard_map/all_gather | solution.py:214
  409.7 456.5 %all-gather.30.cloned.1.call-start = ((), (), s32[]{:S(2)}) async-start(), calls=%async_computation.37 | async-start | bytes 1327104 | tf_op jit(solution)/shard_map/all_gather | solution.py:216
  410.3 498.1 %all-gather.28.cloned.1.call-start = ((), (), s32[]{:S(2)}) async-start(), calls=%async_computation.36 | async-start | bytes 1327104 | tf_op jit(solution)/shard_map/all_gather | solution.py:215
  411.0 558.5 %all-reduce.14.cloned.1.call-start = ((), (), s32[]{:S(2)}) async-start(), calls=%async_computation.18 | async-start | bytes 1572864 | tf_op jit(solution)/shard_map/psum | solution.py:275
  936.0 84.2 %reduce-scatter.52.cloned.1.call-start = ((), (), s32[]{:S(2)}) async-start(), calls=%async_computation.47 | async-start | bytes 442368
  950.0 82.9 %all-reduce.16.cloned.1.call-start = ((), (), s32[]{:S(2)}) async-start(), calls=%async_computation.48 | async-start | bytes 1572864 | tf_op jit(solution)/shard_map/psum | solution.py:229
  978.6 103.5 %reduce-scatter.34.cloned.1.call-start = ((), (), s32[]{:S(2)}) async-start(), calls=%async_computation.26 | async-start | bytes 2654208 | tf_op jit(solution)/shard_map/reduce_scatter | solution.py:263
  980.7 172.8 %reduce-scatter.32.cloned.1.call-start = ((), (), s32[]{:S(2)}) async-start(), calls=%async_computation.25 | async-start | bytes 2654208 | tf_op jit(solution)/shard_map/reduce_scatter | solution.py:263
  983.8 241.3 %reduce-scatter.30.cloned.1.call-start = ((), (), s32[]{:S(2)}) async-start(), calls=%async_computation.24 | async-start | bytes 2654208 | tf_op jit(solution)/shard_map/reduce_scatter | solution.py:263
  987.0 309.7 %reduce-scatter.28.cloned.1.call-start = ((), (), s32[]{:S(2)}) async-start(), calls=%async_computation.23 | async-start | bytes 2654208 | tf_op jit(solution)/shard_map/reduce_scatter | solution.py:263
  990.1 378.0 %reduce-scatter.42.cloned.1.call-start = ((), (), s32[]{:S(2)}) async-start(), calls=%async_computation.30 | async-start | bytes 2654208 | tf_op jit(solution)/shard_map/reduce_scatter | solution.py:264
  993.2 446.2 %reduce-scatter.40.cloned.1.call-start = ((), (), s32[]{:S(2)}) async-start(), calls=%async_computation.29 | async-start | bytes 2654208 | tf_op jit(solution)/shard_map/reduce_scatter | solution.py:264
  996.1 514.6 %reduce-scatter.38.cloned.1.call-start = ((), (), s32[]{:S(2)}) async-start(), calls=%async_computation.28 | async-start | bytes 2654208 | tf_op jit(solution)/shard_map/reduce_scatter | solution.py:264
  999.1 583.0 %reduce-scatter.36.cloned.1.call-start = ((), (), s32[]{:S(2)}) async-start(), calls=%async_computation.27 | async-start | bytes 2654208 | tf_op jit(solution)/shard_map/reduce_scatter | solution.py:264
  1002.0 651.4 %reduce-scatter.50.cloned.1.call-start = ((), (), s32[]{:S(2)}) async-start(), calls=%async_computation.34 | async-start | bytes 2654208 | tf_op jit(solution)/shard_map/reduce_scatter | solution.py:265
  1005.1 719.6 %reduce-scatter.48.cloned.1.call-start = ((), (), s32[]{:S(2)}) async-start(), calls=%async_computation.33 | async-start | bytes 2654208 | tf_op jit(solution)/shard_map/reduce_scatter | solution.py:265
  1008.3 788.0 %reduce-scatter.46.cloned.1.call-start = ((), (), s32[]{:S(2)}) async-start(), calls=%async_computation.32 | async-start | bytes 2654208 | tf_op jit(solution)/shard_map/reduce_scatter | solution.py:265
  1011.4 856.3 %reduce-scatter.44.cloned.1.call-start = ((), (), s32[]{:S(2)}) async-start(), calls=%async_computation.31 | async-start | bytes 2654208 | tf_op jit(solution)/shard_map/reduce_scatter | solution.py:265
  1014.5 918.6 %reduce-scatter.20.cloned.1.call-start = ((), (), s32[]{:S(2)}) async-start(), calls=%async_computation.19 | async-start | bytes 884736 | tf_op jit(solution)/shard_map/reduce_scatter | solution.py:328
  1016.4 982.5 %reduce-scatter.22.cloned.1.call-start = ((), (), s32[]{:S(2)}) async-start(), calls=%async_computation.20 | async-start | bytes 884736 | tf_op jit(solution)/shard_map/reduce_scatter | solution.py:329
  1017.8 1046.5 %reduce-scatter.24.cloned.1.call-start = ((), (), s32[]{:S(2)}) async-start(), calls=%async_computation.21 | async-start | bytes 884736 | tf_op jit(solution)/shard_map/reduce_scatter | solution.py:330
  1019.2 1110.8 %reduce-scatter.26.cloned.1.call-start = ((), (), s32[]{:S(2)}) async-start(), calls=%async_computation.22 | async-start | bytes 884736 | tf_op jit(solution)/shard_map/reduce_scatter | solution.py:331
  (119 other events, 6184.9 us)
Sparse Core Ops, SparseCore 0:
  402.1 31.9 all-reduce.11
  936.2 33.2 all-reduce.13
  978.8 34.9 all-reduce.15
Sparse Core Ops, SparseCore 1:
  405.2 38.8 all-gather.43
  446.1 40.0 all-gather.47
  488.2 40.0 all-gather.45
  530.5 40.0 all-gather.37
  572.7 40.0 all-gather.41
  615.0 40.0 all-gather.39
  657.1 40.0 all-gather.31
  699.1 40.0 all-gather.35
  741.2 40.0 all-gather.33
  784.1 40.0 all-gather.25
  826.2 40.0 all-gather.29
  868.4 40.0 all-gather.27
  950.1 60.3 reduce-scatter.51
  1013.9 68.1 reduce-scatter.33
  1085.6 67.9 reduce-scatter.31
  1157.1 67.9 reduce-scatter.29
  1228.6 67.9 reduce-scatter.27
  1300.1 67.9 reduce-scatter.41
  1371.5 67.8 reduce-scatter.39
  1442.8 67.8 reduce-scatter.37
  1514.1 68.0 reduce-scatter.35
  1585.5 67.9 reduce-scatter.49
  1656.8 67.9 reduce-scatter.47
  1728.3 67.9 reduce-scatter.45
  1799.6 68.0 reduce-scatter.43
  1871.6 61.5 reduce-scatter.19
  1937.4 61.5 reduce-scatter.21
  2002.7 61.5 reduce-scatter.23
  2068.4 61.6 reduce-scatter.25
where the time goes:
time: 2150 us; the launch traced here: 2140 us
  waiting for transfers between devices  1490 us (69%)
  local copies, waits for them, and re-layouts  303 us (14%)
  blocking collectives  208 us (10%)
  matrix products  84.5 us (4%)
  other arithmetic  29 us (1%)
    reduce_scatter x4, waiting for transfers between devices, body(): lax.psum_scatter(grad_down, 'dp', scatter_dimension=0, tiled=True)  283 us
    reduce_scatter x4, waiting for transfers between devices, body(): lax.psum_scatter(grad_up, 'dp', scatter_dimension=0, tiled=True)  283 us
    gather x2, local copies, waits for them, and re-layouts, block_scores(): bias_blk = jnp.take(dist_bias, jnp.clip(offset, 0, seq_len - 1), axis=1)  236 us
    reduce_scatter x4, waiting for transfers between devices, body(): lax.psum_scatter(grad_gate, 'dp', scatter_dimension=0, tiled=True)  221 us
    all_gather x4, waiting for transfers between devices, body(): lax.all_gather(w_up[expert], 'dp', axis=0, tiled=True)  155 us
    all_gather x4, waiting for transfers between devices, body(): lax.all_gather(w_down_t[expert], 'dp', axis=0, tiled=True)  151 us
    all_gather x4, waiting for transfers between devices, body(): lax.all_gather(w_gate[expert], 'dp', axis=0, tiled=True)  114 us
    reduce_scatter x1, waiting for transfers between devices, body(): lax.psum_scatter(grad_key, 'dp', scatter_dimension=0, tiled=True)  65.8 us
  transfers between devices with their start and end apart: 32, of which 28 were waited for; matrix products, arithmetic and copies ran while one was open for 6% of the time, Pallas kernels for 0%

commit v1 on v0

v1 whole, which is shorter than its diff:
```python
import functools

import jax
import jax.numpy as jnp
from jax import lax
from jax.experimental import pallas as pl
from jax.experimental.pallas import tpu as pltpu
from jax.sharding import PartitionSpec as P

DH = 64
CAP = 144
EPSILON = 1e-06
NEG_FILL = -1e30
HIGHEST = lax.Precision.HIGHEST
BF = jnp.bfloat16
F32 = jnp.float32
VMEM_LIMIT = 48 * 1024 * 1024


def mm(a, b, ca=1, cb=0):
    return lax.dot_general(a, b, (((ca,), (cb,)), ((), ())), preferred_element_type=F32)


def exchange_kernel(axis, n, kinds, *refs):
    m = len(kinds)
    ins, outs = refs[:m], refs[m : 2 * m]
    local_sem, send_sem, recv_sem = refs[2 * m :]
    me = lax.axis_index(axis)
    barrier = pltpu.get_barrier_semaphore()

    def greet(k, carry):
        pl.semaphore_signal(
            barrier,
            inc=1,
            device_id={axis: lax.rem(me + k, n)},
            device_id_type=pl.DeviceIdType.MESH,
        )
        return carry

    lax.fori_loop(1, n, greet, 0)

    def source(a, target):
        return ins[a] if kinds[a] == 0 else ins[a].at[target // kinds[a]]

    locals_ = [
        pltpu.make_async_copy(source(a, me), outs[a].at[me], local_sem.at[a]) for a in range(m)
    ]
    for copy in locals_:
        copy.start()
    pl.semaphore_wait(barrier, n - 1)

    def remote(a, k):
        target = lax.rem(me + k, n)
        return pltpu.make_async_remote_copy(
            src_ref=source(a, target),
            dst_ref=outs[a].at[me],
            send_sem=send_sem.at[a, k],
            recv_sem=recv_sem.at[a, k],
            device_id={axis: target},
            device_id_type=pl.DeviceIdType.MESH,
        )

    for a in range(m):

        def start(k, carry, a=a):
            remote(a, k).start()
            return carry

        lax.fori_loop(1, n, start, 0)
    for copy in locals_:
        copy.wait()
    for a in range(m):

        def finish(k, carry, a=a):
            remote(a, k).wait()
            return carry

        lax.fori_loop(1, n, finish, 0)


def exchange(arrays, kinds, axis, n, cid):
    m = len(arrays)
    shapes = [
        jax.ShapeDtypeStruct((n,) + (a.shape if k == 0 else a.shape[1:]), a.dtype)
        for a, k in zip(arrays, kinds)
    ]
    return pl.pallas_call(
        functools.partial(exchange_kernel, axis, n, kinds),
        out_shape=shapes,
        in_specs=[pl.BlockSpec(memory_space=pl.ANY)] * m,
        out_specs=[pl.BlockSpec(memory_space=pl.ANY)] * m,
        scratch_shapes=[
            pltpu.SemaphoreType.DMA((m,)),
            pltpu.SemaphoreType.DMA((m, n)),
            pltpu.SemaphoreType.DMA((m, n)),
        ],
        compiler_params=pltpu.CompilerParams(collective_id=cid, has_side_effects=True),
    )(*arrays)


def skew(x, forward):
    size = x.shape[1]
    row = lax.broadcasted_iota(jnp.int32, x.shape, 0)
    step = 1
    while step < size:
        rolled = pltpu.roll(x, step if forward else size - step, 1)
        x = jnp.where((row & step) != 0, rolled, x)
        step *= 2
    return x


def attn_fwd_kernel(q_ref, seg_row_ref, seg_col_ref, dist_ref, mixed_ref, prob_ref):
    n_heads, size = dist_ref.shape
    width = n_heads * DH
    shape = (size, size)
    row = lax.broadcasted_iota(jnp.int32, shape, 0)
    col = lax.broadcasted_iota(jnp.int32, shape, 1)
    allowed = (col <= row) & (seg_col_ref[...] == seg_row_ref[...])
    for h in range(n_heads):
        q = q_ref[:, h * DH : (h + 1) * DH]
        k = q_ref[:, width + h * DH : width + (h + 1) * DH]
        v = q_ref[:, 2 * width + h * DH : 2 * width + (h + 1) * DH]
        bias = skew(jnp.broadcast_to(dist_ref[h : h + 1, :], shape), True)
        scores = jnp.where(allowed, mm(q, k, 1, 1) * DH ** (-0.5) + bias, NEG_FILL)
        top = jnp.max(scores, axis=1, keepdims=True)
        e = jnp.exp(scores - top)
        prob = e / jnp.sum(e, axis=1, keepdims=True)
        prob_ref[h] = prob
        mixed_ref[:, h * DH : (h + 1) * DH] = mm(prob.astype(BF), v).astype(BF)


def attn_bwd_kernel(q_ref, prob_ref, dmix_ref, dq_ref, dist_ref):
    n_heads, size = dist_ref.shape
    width = n_heads * DH
    scale = DH ** (-0.5)
    for h in range(n_heads):
        q = q_ref[:, h * DH : (h + 1) * DH]
        k = q_ref[:, width + h * DH : width + (h + 1) * DH]
        v = q_ref[:, 2 * width + h * DH : 2 * width + (h + 1) * DH]
        dm = dmix_ref[:, h * DH : (h + 1) * DH]
        prob = prob_ref[h]
        d_prob = mm(dm, v, 1, 1)
        ds = prob * (d_prob - jnp.sum(prob * d_prob, axis=1, keepdims=True))
        low = ds.astype(BF)
        dq_ref[:, h * DH : (h + 1) * DH] = (mm(low, k) * scale).astype(BF)
        dq_ref[:, width + h * DH : width + (h + 1) * DH] = (mm(low, q, 0, 0) * scale).astype(BF)
        dq_ref[:, 2 * width + h * DH : 2 * width + (h + 1) * DH] = mm(
            prob.astype(BF), dm, 0, 0
        ).astype(BF)
        dist_ref[h : h + 1, :] = jnp.sum(skew(ds, False), axis=0, keepdims=True)


def local_call(kernel, out_shape, *args):
    return pl.pallas_call(
        kernel,
        out_shape=out_shape,
        compiler_params=pltpu.CompilerParams(vmem_limit_bytes=VMEM_LIMIT),
    )(*args)


def rms_scale(values, gain_vec):
    inverse = lax.rsqrt(jnp.mean(values * values, axis=-1, keepdims=True) + EPSILON)
    return values * inverse * gain_vec


def gated_unit(gate_act, up_act):
    return jax.nn.gelu(gate_act, approximate=False) * up_act


def soft_router(logits):
    return jax.nn.softmax(logits, axis=-1)


def body(
    n_dp,
    n_t,
    tokens,
    cotangent,
    segment_ids,
    routes,
    buckets,
    gain_attn,
    w_query,
    w_key,
    w_value,
    w_out_t,
    gain_moe,
    w_router,
    w_gate,
    w_up,
    w_down_t,
    bias_table,
):
    seq, width = tokens.shape
    n_exp, d_rows, hidden = w_gate.shape
    n_heads, n_buckets = bias_table.shape
    cols = n_heads * DH
    cuts = n_dp // n_exp
    part = hidden // cuts
    SDS = jax.ShapeDtypeStruct

    packed = jnp.concatenate([w_query, w_key, w_value, w_out_t], axis=1)
    smalls = jnp.concatenate(
        [gain_attn[None], gain_moe[None], w_router.T, jnp.zeros((2, d_rows), BF)], axis=0
    )
    experts_out = (
        jnp.stack([w_gate, w_up, w_down_t])
        .reshape(3, n_exp, d_rows, cuts, part)
        .transpose(1, 3, 0, 2, 4)
        .reshape(n_dp, 3, d_rows, part)
    )
    full, small_full, experts_in = exchange(
        [packed, smalls, experts_out], (0, 0, 1), "dp", n_dp, 0
    )
    full = full.reshape(width, 4 * cols)
    w_qkv, w_out = full[:, : 3 * cols], full[:, 3 * cols :]
    small_full = small_full.transpose(1, 0, 2).reshape(8, width)
    attn_gain_f = small_full[0].astype(F32)
    moe_gain_f = small_full[1].astype(F32)
    router_t = small_full[2 : 2 + n_exp]
    e_gate, e_up, e_down = [experts_in[:, i].reshape(width, part) for i in range(3)]

    token_f = tokens.astype(F32)
    normed = rms_scale(token_f, attn_gain_f).astype(BF)
    qkv = mm(normed, w_qkv).astype(BF)
    buckets_rev = jnp.roll(jnp.flip(buckets), 1)
    dist_hot = (buckets_rev[:, None] == jnp.arange(n_buckets, dtype=jnp.int32)[None, :]).astype(F32)
    dist_bias = jnp.dot(bias_table.astype(F32), dist_hot.T, precision=HIGHEST)
    mixed, prob = local_call(
        attn_fwd_kernel,
        [SDS((seq, cols), BF), SDS((n_heads, seq, seq), F32)],
        qkv,
        segment_ids,
        segment_ids.reshape(seq, 1),
        dist_bias,
    )
    attn_part = mm(mixed, w_out, 1, 1).astype(BF)
    (attn_parts,) = exchange([attn_part], (0,), "tensor", n_t, 1)
    residual = token_f + jnp.sum(attn_parts.astype(F32), axis=0)
    normed_moe = rms_scale(residual, moe_gain_f).astype(BF)
    logits = mm(normed_moe, router_t, 1, 1)
    router = soft_router(logits)

    expert_ids = jnp.arange(n_exp, dtype=jnp.int32)
    chosen = jnp.any(routes[:, :, None] == expert_ids[None, None, :], axis=1)
    chosen_b = chosen.astype(BF)
    position = jnp.arange(seq, dtype=jnp.int32)
    lower = (position[:, None] >= position[None, :]).astype(BF)
    place = mm(lower, chosen_b).astype(jnp.int32) - 1
    place = jnp.where(chosen, place, -1)
    slot_ids = jnp.arange(CAP, dtype=jnp.int32)
    pick = (place.T[:, None, :] == slot_ids[None, :, None]).astype(BF)
    gates = router * chosen.astype(F32)
    grad_final = cotangent.astype(F32)
    d_rows_all = (gates.T[:, :, None] * grad_final[None]).astype(BF)
    rows_all = jnp.concatenate(
        [jnp.broadcast_to(normed_moe[None], (n_exp, seq, width)), d_rows_all], axis=2
    )
    sends = jnp.einsum("est,etd->esd", pick, rows_all, preferred_element_type=F32).astype(BF)
    (arrived,) = exchange([sends], (cuts,), "dp", n_dp, 2)
    arrived = arrived.reshape(n_dp * CAP, 2 * width)
    rows_x, rows_d = arrived[:, :width], arrived[:, width:]

    gate_act = mm(rows_x, e_gate)
    up_act = mm(rows_x, e_up)
    inner, unit_pull = jax.vjp(gated_unit, gate_act, up_act)
    inner = inner.astype(BF)
    d_inner = mm(rows_d, e_down)
    d_gate_act, d_up_act = unit_pull(d_inner)
    d_gate_act, d_up_act = d_gate_act.astype(BF), d_up_act.astype(BF)
    part_out = mm(inner, e_down, 1, 1).astype(BF)
    part_dx = (mm(d_gate_act, e_gate, 1, 1) + mm(d_up_act, e_up, 1, 1)).astype(BF)
    returns = jnp.concatenate([part_out, part_dx], axis=1).reshape(n_dp, CAP, 2 * width)
    (returned,) = exchange([returns], (1,), "dp", n_dp, 3)
    g_down = mm(rows_d, inner, 0, 0).astype(BF)
    g_gate = mm(rows_x, d_gate_act, 0, 0).astype(BF)
    g_up = mm(rows_x, d_up_act, 0, 0).astype(BF)

    returned = returned.reshape(n_exp, cuts * CAP, 2 * width)
    pick_back = jnp.tile(pick, (1, cuts, 1))
    home = jnp.einsum("est,esd->etd", pick_back, returned, preferred_element_type=F32)
    moe_part = jnp.sum(gates.T[:, :, None] * home[:, :, :width], axis=0).astype(BF)
    d_moe_part = jnp.sum(home[:, :, width:], axis=0).astype(BF)
    d_router_part = jnp.sum(home[:, :, :width] * grad_final[None], axis=2)
    moe_parts, d_moe_parts, d_router_parts = exchange(
        [moe_part, d_moe_part, d_router_part], (0, 0, 0), "tensor", n_t, 4
    )
    moe_out = jnp.sum(moe_parts.astype(F32), axis=0)
    d_moe = jnp.sum(d_moe_parts.astype(F32), axis=0)
    d_router = jnp.sum(d_router_parts, axis=0).T
    output = (residual + moe_out).astype(BF)

    unused, soft_pull = jax.vjp(soft_router, logits)
    d_logits = soft_pull(d_router)[0].astype(BF)
    g_router = mm(d_logits, normed_moe, 0, 0)
    d_normed_moe = d_moe + mm(d_logits, router_t)
    unused, moe_pull = jax.vjp(rms_scale, residual, moe_gain_f)
    d_resid_norm, g_moe_gain = moe_pull(d_normed_moe)
    d_residual = grad_final + d_resid_norm
    d_branch = d_residual.astype(BF)
    g_out = mm(d_branch, mixed, 0, 0)
    d_mixed = mm(d_branch, w_out).astype(BF)
    d_qkv, d_dist = local_call(
        attn_bwd_kernel,
        [SDS((seq, 3 * cols), BF), SDS((n_heads, seq), F32)],
        qkv,
        prob,
        d_mixed,
    )
    g_table = jnp.dot(d_dist, dist_hot, precision=HIGHEST)
    d_normed_part = mm(d_qkv, w_qkv, 1, 1).astype(BF)
    (d_normed_parts,) = exchange([d_normed_part], (0,), "tensor", n_t, 5)
    d_normed = jnp.sum(d_normed_parts.astype(F32), axis=0)
    g_qkv = mm(normed, d_qkv, 0, 0)
    unused, first_pull = jax.vjp(rms_scale, token_f, attn_gain_f)
    d_token_norm, g_attn_gain = first_pull(d_normed)
    grad_tokens = (d_residual + d_token_norm).astype(BF)

    g_attn = jnp.concatenate([g_qkv, g_out], axis=1).astype(BF).reshape(n_dp, d_rows, 4 * cols)
    g_small = jnp.concatenate(
        [g_attn_gain[None], g_moe_gain[None], g_router, jnp.zeros((2, width), F32)], axis=0
    )
    g_small = g_small.reshape(8, n_dp, d_rows).transpose(1, 0, 2)
    g_exp = jnp.stack([g.reshape(n_dp, d_rows, part) for g in (g_gate, g_up, g_down)], axis=1)
    r_attn, r_small, r_exp, r_table = exchange(
        [g_attn, g_small, g_exp, g_table], (1, 1, 1, 0), "dp", n_dp, 6
    )
    attn_total = jnp.sum(r_attn.astype(F32), axis=0)
    small_total = jnp.sum(r_small, axis=0)
    exp_total = (
        r_exp.reshape(n_exp, cuts, 3, d_rows, part)
        .transpose(2, 0, 3, 1, 4)
        .reshape(3, n_exp, d_rows, hidden)
        .astype(F32)
    )
    return (
        output,
        grad_tokens,
        small_total[0],
        attn_total[:, :cols],
        attn_total[:, cols : 2 * cols],
        attn_total[:, 2 * cols : 3 * cols],
        attn_total[:, 3 * cols :],
        small_total[1],
        small_total[2 : 2 + n_exp].T,
        exp_total[0],
        exp_total[1],
        exp_total[2],
        jnp.sum(r_table, axis=0),
    )


def solution(mesh):
    row, both, expert = P("dp", None), P("dp", "tensor"), P(None, "dp", "tensor")
    table = P("tensor", None)
    in_specs = (row, row, row, row, P(), P("dp"), both, both, both, both, P("dp"), row)
    in_specs = in_specs + (expert, expert, expert, table)
    out_specs = (row, row, P("dp"), both, both, both, both, P("dp"), row)
    out_specs = out_specs + (expert, expert, expert, table)
    return jax.shard_map(
        functools.partial(body, mesh.shape["dp"], mesh.shape["tensor"]),
        mesh=mesh,
        in_specs=in_specs,
        out_specs=out_specs,
        check_vma=False,
    )
```

time: 2150 us -> 486 us (0.23)
  waiting for transfers between devices: 1490 us -> 0 us
  Pallas kernels: 0 us -> 385 us
  local copies, waits for them, and re-layouts: 303 us -> 37.8 us
  blocking collectives: 208 us -> 0 us
  matrix products: 84.5 us -> 33.4 us
    reduce_scatter x16 -> x0, waiting for transfers between devices: 1050 us -> none  [the longest x4 283 us: body(): lax.psum_scatter(grad_down, 'dp', scatter_dimension=0, tiled=True)]
    all_gather x12 -> x0, waiting for transfers between devices: 420 us -> none  [the longest x4 155 us: body(): lax.all_gather(w_up[expert], 'dp', axis=0, tiled=True)]
    pallas_call x0 -> x9, Pallas kernels: none -> 385 us  [the longest x7 379 us: exchange(): pl.pallas_call(functools.partial(exchange_kernel, axis, n, kinds), out_sh...]
    gather x17 -> x0, local copies, waits for them, and re-layouts: 257 us -> none  [the longest x2 236 us: block_scores(): bias_blk = jnp.take(dist_bias, jnp.clip(offset, 0, seq_len - 1), axis=1)]
    all_gather x5 -> x0, blocking collectives: 143 us -> none  [the longest x1 33 us: body(): lax.all_gather(w_value, 'dp', axis=0, tiled=True)]
    unnamed x2 -> x0, blocking collectives: 59 us -> none
    dot_general x58 -> x23, matrix products: 83.4 us -> 33.4 us  [the longest x19 26.7 us: mm(): lax.dot_general(a, b, (((ca,), (cb,)), ((), ())), preferred_element_type=...]
    unnamed x252 -> x46, local copies, waits for them, and re-layouts: 26 us -> 2.78 us
  transfers between devices with their start and end apart: 32 -> 0, of which waited for: 28 -> 0; matrix products, arithmetic and copies ran while one was open for 6% -> 0% of each run, Pallas kernels for 0% -> 0%
where the time goes in v1:
time: 486 us; the launch traced here: 485 us
  Pallas kernels  385 us (79%)
  local copies, waits for them, and re-layouts  37.8 us (8%)
  matrix products  33.4 us (7%)
  other arithmetic  28.2 us (6%)
    pallas_call x7, Pallas kernels, exchange(): pl.pallas_call(functools.partial(exchange_kernel, axis, n, kinds), out_sh...  379 us
    dot_general x19, matrix products, mm(): lax.dot_general(a, b, (((ca,), (cb,)), ((), ())), preferred_element_type=...  26.7 us

profile of v1, /device:TPU:0, one launch (start us, length us, event | category | flops | bytes accessed | tf_op | source)
XLA Modules:
  0.0 485.3 jit_solution(17342209094413260477)
XLA Ops:
  0.7 1.9 stack.15
  6.9 57.3 %shard_map.255 = (bf16[8,96,768]{2,1,0:T(8,128)(2,1)}, bf16[8,8,96]{2,1,0:T(8,128)(2,1)}, bf16[8,3,96,384]{3,2,1,0:T(8,128)(2,1)}) custom-call(bf16[96,768]{1,0:T(8,128)(2,1)} %pad_maximum_fusion.4.refs_0_, bf16[8,96]{1,0:T(8,128)(2,1)} %maximum_maximum_fusion.refs_1_, bf16[8,3,96,384]{3,2,1,0:T(8,128)(2,1)} %bitcast.79), custom_call_target="tpu_custom_call" | custom-call | tf_op jit(solution)/shard_map/pallas_call | solution.py:87
  65.3 1.7 convolution_convert_fusion.6.q_ref
  68.9 2.9 shard_map.256
  71.8 2.1 convolution_convert_fusion.5.refs_0_
  73.9 19.3 %shard_map.257 = bf16[4,256,768]{2,1,0:T(8,128)(2,1)} custom-call(bf16[256,768]{1,0:T(8,128)(2,1)} %convolution_convert_fusion.5.refs_0_), custom_call_target="tpu_custom_call" | custom-call | tf_op jit(solution)/shard_map/pallas_call | solution.py:87
  98.1 1.9 fusion.5.refs_0_
  100.0 75.6 %shard_map.258 = bf16[8,144,1536]{2,1,0:T(8,128)(2,1)} custom-call(bf16[4,144,1536]{2,1,0:T(8,128)(2,1)} %fusion.5.refs_0_), custom_call_target="tpu_custom_call" | custom-call | tf_op jit(solution)/shard_map/pallas_call | solution.py:87
  175.6 1.8 fusion.62
  179.2 5.2 %multiply_convert_fusion.2 = (bf16[1152,384]{1,0:T(8,128)(2,1)S(1)}, f32[1152,384]{1,0:T(8,128)S(1)}, f32[1152,384]{1,0:T(8,128)S(1)}) fusion(f32[1152,384]{1,0:T(8,128)S(1)} %fusion.25, bf16[768,384]{1,0:T(8,128)(2,1)S(1)} %bitcast.88, bf16[1152,1536]{1,0:T(8,128)(2,1)S(1)} %bitcast.83), kind=kOutput, calls=%fused_computation.25 | convolution fusion | flops 708673536 | bytes 8552448 | tf_op jit(solution)/shard_map/dot_general | solution.py:21
  184.4 1.7 multiply_convert_fusion.1
  194.7 2.1 pad_maximum_fusion
  196.8 5.7 %copy.76 = bf16[1152,1536]{1,0:T(8,128)(2,1)} copy(bf16[1152,1536]{0,1:T(8,128)(2,1)} %pad_maximum_fusion) | data formatting | bytes 7077888 | tf_op jit(solution)/shard_map/concatenate | solution.py:273
  202.6 80.6 %shard_map.259 = bf16[8,144,1536]{2,1,0:T(8,128)(2,1)} custom-call(bf16[8,144,1536]{2,1,0:T(8,128)(2,1)} %bitcast.78), custom_call_target="tpu_custom_call" | custom-call | tf_op jit(solution)/shard_map/pallas_call | solution.py:87
  283.3 3.8 fusion.69
  287.2 2.0 multiply_reduce_fusion
  289.2 37.4 %shard_map.260 = (bf16[4,256,768]{2,1,0:T(8,128)(2,1)}, bf16[4,256,768]{2,1,0:T(8,128)(2,1)}, f32[4,4,256]{2,1,0:T(4,128)}) custom-call(bf16[256,768]{1,0:T(8,128)(2,1)} %get-tuple-element.43.refs_0_, bf16[256,768]{1,0:T(8,128)(2,1)} %get-tuple-element.42.refs_1_, f32[4,256]{1,0:T(4,128)} %get-tuple-element.41.refs_2_), custom_call_target="tpu_custom_call" | custom-call | tf_op jit(solution)/shard_map/pallas_call | solution.py:87
  328.6 2.6 convert_reduce_fusion.1
  334.9 2.9 shard_map.261
  337.8 2.5 convolution_convert_fusion.4.refs_0_
  340.2 18.4 %shard_map.262 = bf16[4,256,768]{2,1,0:T(8,128)(2,1)} custom-call(bf16[256,768]{1,0:T(8,128)(2,1)} %convolution_convert_fusion.4.refs_0_), custom_call_target="tpu_custom_call" | custom-call | tf_op jit(solution)/shard_map/pallas_call | solution.py:87
  358.6 1.7 convert_reduce_fusion
  363.0 2.2 copy.78
  365.6 2.4 pad_maximum_fusion.3.refs_0_
  368.9 90.3 %shard_map.263 = (bf16[8,96,768]{2,1,0:T(8,128)(2,1)}, f32[8,8,96]{2,1,0:T(8,128)}, bf16[8,3,96,384]{3,2,1,0:T(8,128)(2,1)}, f32[8,3,32]{2,1,0:T(4,128)}) custom-call(bf16[8,96,768]{2,1,0:T(8,128)(2,1)} %pad_maximum_fusion.3.refs_0_, f32[8,8,96]{2,1,0:T(8,128)} %maximum_bitcast_fusion.refs_1_, bf16[8,3,96,384]{3,2,1,0:T(8,128)(2,1)} %pad_maximum_fusion.2.refs_2_, ...), custom_call_target="tpu_custom_call" | custom-call | tf_op jit(solution)/shard_map/pallas_call | solution.py:87
  459.2 1.9 convert_bitcast_fusion
  462.8 1.9 copy.81
  464.7 3.1 squeeze.19
  467.8 3.2 copy.82
  471.0 3.1 squeeze.20
  474.0 3.2 copy.83
  477.2 3.1 squeeze.21
  (122 shorter events, 38.6 us)
Async XLA Ops:
  0.6 67.9 %copy-start = (bf16[3,32]{1,0:T(4,128)(2,1)S(1)}, bf16[3,32]{1,0:T(4,128)(2,1)}, u32[]{:S(2)}) copy-start(bf16[3,32]{1,0:T(4,128)(2,1)} %param.31) | copy-start | bytes 580
  0.7 2.0 copy-start.8
  2.6 1.1 copy-start.9
  3.9 1.5 copy-start.10
  3.9 1.5 copy-start.11
  3.9 1.5 copy-start.12
  3.9 1.5 copy-start.13
  3.9 2.4 copy-start.19
  3.9 2.3 copy-start.20
  3.9 2.3 copy-start.21
  5.4 59.7 %copy-start.3 = (bf16[256,768]{1,0:T(8,128)(2,1)S(1)}, bf16[256,768]{1,0:T(8,128)(2,1)}, u32[]{:S(2)}) copy-start(bf16[256,768]{1,0:T(8,128)(2,1)} %param.16) | copy-start | bytes 1179652
  64.2 2.8 copy-start.18
  64.2 4.5 copy-start.2
  95.0 0.7 copy-start.16
  95.0 1.1 copy-start.17
  95.7 0.7 copy-start.4
  96.4 1.4 copy-start.5
  175.6 2.5 copy-start.6
  331.2 1.0 copy-start.7
  477.2 5.4 %copy-start.14 = (f32[8,8,96]{2,1,0:T(8,128)S(1)}, f32[8,8,96]{2,1,0:T(8,128)}, u32[]{:S(2)}) copy-start(f32[8,8,96]{2,1,0:T(8,128)} %get-tuple-element.37) | copy-start | bytes 73732
  477.2 6.5 %copy-start.15 = (f32[8,3,32]{2,1,0:T(4,128)S(1)}, f32[8,3,32]{2,1,0:T(4,128)}, u32[]{:S(2)}) copy-start(f32[8,3,32]{2,1,0:T(4,128)} %get-tuple-element.40) | copy-start | bytes 9220
  480.3 5.0 %copy-start.1 = (bf16[3,32]{1,0:T(4,128)(2,1)S(1)}, bf16[3,32]{1,0:T(4,128)(2,1)}, u32[]{:S(2)}) copy-start(bf16[3,32]{1,0:T(4,128)(2,1)} %param.31) | copy-start | bytes 580

commit v2 on v1

--- a/solution.py
+++ b/solution.py
@@ -21,81 +21,270 @@
     return lax.dot_general(a, b, (((ca,), (cb,)), ((), ())), preferred_element_type=F32)
 
 
-def exchange_kernel(axis, n, kinds, *refs):
+MESH = pl.DeviceIdType.MESH
+
+
+def greet(barrier, axis, n):
+    me = lax.axis_index(axis)
+
+    def one(k, carry):
+        target = lax.rem(me + k, n)
+        pl.semaphore_signal(barrier, inc=1, device_id={axis: target}, device_id_type=MESH)
+        return carry
+
+    lax.fori_loop(1, n, one, 0)
+    return n - 1
+
+
+def each(start, stop, action):
+    def one(k, carry):
+        action(k)
+        return carry
+
+    lax.fori_loop(start, stop, one, 0)
+
+
+def exchange_kernel(sizes, kinds, axes, *refs):
     m = len(kinds)
     ins, outs = refs[:m], refs[m : 2 * m]
     local_sem, send_sem, recv_sem = refs[2 * m :]
-    me = lax.axis_index(axis)
     barrier = pltpu.get_barrier_semaphore()
-
-    def greet(k, carry):
-        pl.semaphore_signal(
-            barrier,
-            inc=1,
-            device_id={axis: lax.rem(me + k, n)},
-            device_id_type=pl.DeviceIdType.MESH,
-        )
-        return carry
-
-    lax.fori_loop(1, n, greet, 0)
+    expected = 0
+    for axis in sorted(set(axes)):
+        expected += greet(barrier, axis, sizes[axis])
+    places = [lax.axis_index(axis) for axis in axes]
 
     def source(a, target):
         return ins[a] if kinds[a] == 0 else ins[a].at[target // kinds[a]]
 
     locals_ = [
-        pltpu.make_async_copy(source(a, me), outs[a].at[me], local_sem.at[a]) for a in range(m)
+        pltpu.make_async_copy(source(a, places[a]), outs[a].at[places[a]], local_sem.at[a])
+        for a in range(m)
     ]
     for copy in locals_:
         copy.start()
-    pl.semaphore_wait(barrier, n - 1)
+    pl.semaphore_wait(barrier, expected)
 
     def remote(a, k):
-        target = lax.rem(me + k, n)
+        target = lax.rem(places[a] + k, sizes[axes[a]])
         return pltpu.make_async_remote_copy(
             src_ref=source(a, target),
-            dst_ref=outs[a].at[me],
+            dst_ref=outs[a].at[places[a]],
             send_sem=send_sem.at[a, k],
             recv_sem=recv_sem.at[a, k],
-            device_id={axis: target},
-            device_id_type=pl.DeviceIdType.MESH,
+            device_id={axes[a]: target},
+            device_id_type=MESH,
         )
 
     for a in range(m):
-
-        def start(k, carry, a=a):
-            remote(a, k).start()
-            return carry
-
-        lax.fori_loop(1, n, start, 0)
+        each(1, sizes[axes[a]], lambda k, a=a: remote(a, k).start())
     for copy in locals_:
         copy.wait()
     for a in range(m):
-
-        def finish(k, carry, a=a):
-            remote(a, k).wait()
-            return carry
-
-        lax.fori_loop(1, n, finish, 0)
-
-
-def exchange(arrays, kinds, axis, n, cid):
+        each(1, sizes[axes[a]], lambda k, a=a: remote(a, k).wait())
+
+
+def exchange(sizes, arrays, kinds, axes, cid):
     m = len(arrays)
+    most = max(sizes[axis] for axis in axes)
     shapes = [
-        jax.ShapeDtypeStruct((n,) + (a.shape if k == 0 else a.shape[1:]), a.dtype)
-        for a, k in zip(arrays, kinds)
+        jax.ShapeDtypeStruct((sizes[axis],) + (a.shape if k == 0 else a.shape[1:]), a.dtype)
+        for a, k, axis in zip(arrays, kinds, axes)
     ]
     return pl.pallas_call(
-        functools.partial(exchange_kernel, axis, n, kinds),
+        functools.partial(exchange_kernel, sizes, kinds, axes),
         out_shape=shapes,
         in_specs=[pl.BlockSpec(memory_space=pl.ANY)] * m,
         out_specs=[pl.BlockSpec(memory_space=pl.ANY)] * m,
         scratch_shapes=[
             pltpu.SemaphoreType.DMA((m,)),
-            pltpu.SemaphoreType.DMA((m, n)),
-            pltpu.SemaphoreType.DMA((m, n)),
+            pltpu.SemaphoreType.DMA((m, most)),
+            pltpu.SemaphoreType.DMA((m, most)),
         ],
         compiler_params=pltpu.CompilerParams(collective_id=cid, has_side_effects=True),
     )(*arrays)
+
+
+def relay_setup(n):
+    me, t = lax.axis_index("dp"), lax.axis_index("tensor")
+    pair = t + 1 - 2 * lax.rem(t, 2)
+    across = lax.rem(t + 2, 4)
+    barrier = pltpu.get_barrier_semaphore()
+    for target in (pair, across):
+        pl.semaphore_signal(barrier, inc=1, device_id={"tensor": target}, device_id_type=MESH)
+    return me, t, pair, across, barrier, 2 + greet(barrier, "dp", n)
+
+
+def push(src, dst, sems, index, device):
+    return pltpu.make_async_remote_copy(
+        src_ref=src,
+        dst_ref=dst,
+        send_sem=sems[0].at[index],
+        recv_sem=sems[1].at[index],
+        device_id=device,
+        device_id_type=MESH,
+    )
+
+
+def dispatch_kernel(n, cuts, in_ref, out_ref, local_sem, *sems):
+    me, t, pair, across, barrier, expected = relay_setup(n)
+    ring, over, near, far = [(sems[2 * i], sems[2 * i + 1]) for i in range(4)]
+    own = pltpu.make_async_copy(in_ref.at[me // cuts], out_ref.at[t, me], local_sem)
+    own.start()
+    pl.semaphore_wait(barrier, expected)
+
+    def first(k):
+        target = lax.rem(me + k, n)
+        return push(in_ref.at[target // cuts], out_ref.at[t, me], ring, k, {"dp": target})
+
+    def place(k):
+        return lax.rem(me - k + n, n)
+
+    def cross(k):
+        here = out_ref.at[t, place(k)]
+        return push(here, here, over, k, {"tensor": across})
+
+    def swap(k):
+        here = out_ref.at[t, place(k)]
+        return push(here, here, near, k, {"tensor": pair})
+
+    def forward(k):
+        here = out_ref.at[across, place(k)]
+        return push(here, here, far, k, {"tensor": pair})
+
+    def spread(k):
+        cross(k).start()
+        swap(k).start()
+
+    def hand_on(k):
+        cross(k).wait_recv()
+        forward(k).start()
+
+    each(1, n, lambda k: first(k).start())
+    own.wait()
+    spread(0)
+
+    def step(k):
+        first(k).wait_recv()
+        spread(k)
+        hand_on(k - 1)
+
+    each(1, n, step)
+    hand_on(n - 1)
+    each(1, n, lambda k: first(k).wait_send())
+
+    def finish(k):
+        cross(k).wait_send()
+        swap(k).wait()
+        forward(k).wait()
+
+    each(0, n, finish)
+
+
+def dispatch(sends, n, cuts, cid):
+    _, rows, columns = sends.shape
+    return pl.pallas_call(
+        functools.partial(dispatch_kernel, n, cuts),
+        out_shape=jax.ShapeDtypeStruct((4, n, rows, columns), sends.dtype),
+        in_specs=[pl.BlockSpec(memory_space=pl.ANY)],
+        out_specs=pl.BlockSpec(memory_space=pl.ANY),
+        scratch_shapes=[pltpu.SemaphoreType.DMA] + [pltpu.SemaphoreType.DMA((n,))] * 8,
+        compiler_params=pltpu.CompilerParams(collective_id=cid, has_side_effects=True),
+    )(sends)
+
+
+def return_kernel(n, in_ref, out_ref, held, pair_in, across_in, local_sem, *sems):
+    me, t, pair, across, barrier, expected = relay_setup(n)
+    near, far, over, ring = [(sems[2 * i], sems[2 * i + 1]) for i in range(4)]
+    loads = [
+        pltpu.make_async_copy(in_ref.at[t], held.at[0], local_sem.at[0]),
+        pltpu.make_async_copy(in_ref.at[across], held.at[1], local_sem.at[1]),
+    ]
+    for load in loads:
+        load.start()
+    pl.semaphore_wait(barrier, expected)
+    beyond = lax.rem(pair + 2, 4)
+
+    def place(k):
+        return lax.rem(me + 1 + k, n)
+
+    def share(k):
+        s = place(k)
+        return push(in_ref.at[pair, s], pair_in.at[0, s], near, k, {"tensor": pair})
+
+    def share_far(k):
+        s = place(k)
+        return push(in_ref.at[beyond, s], pair_in.at[1, s], far, k, {"tensor": pair})
+
+    def cross(k):
+        s = place(k)
+        return push(held.at[1, s], across_in.at[s], over, k, {"tensor": across})
+
+    def home(k):
+        s = place(k)
+        return push(held.at[0, s], out_ref.at[me], ring, k, {"dp": s})
+
+    def begin(k):
+        share_far(k).start()
+        share(k).start()
+
+    def sum_far(k):
+        s = place(k)
+        share_far(k).wait_recv()
+        held[1, s] = (held[1, s].astype(F32) + pair_in[1, s].astype(F32)).astype(BF)
+        cross(k).start()
+
+    def sum_own(k):
+        s = place(k)
+        share(k).wait_recv()
+        cross(k).wait_recv()
+        total = held[0, s].astype(F32) + pair_in[0, s].astype(F32) + across_in[s].astype(F32)
+        held[0, s] = total.astype(BF)
+
+    each(0, n, begin)
+    for load in loads:
+        load.wait()
+    sum_far(0)
+
+    def step(k):
+        sum_far(k)
+        sum_own(k - 1)
+        home(k - 1).start()
+
+    each(1, n, step)
+    sum_own(n - 1)
+    own = pltpu.make_async_copy(held.at[0, me], out_ref.at[me], local_sem.at[0])
+    own.start()
+    own.wait()
+    each(0, n - 1, lambda k: home(k).wait())
+
+    def finish(k):
+        share(k).wait_send()
+        share_far(k).wait_send()
+        cross(k).wait_send()
+
+    each(0, n, finish)
+
+
+def send_home(parts, n, cid):
+    _, _, rows, columns = parts.shape
+    block = (n, rows, columns)
+    return pl.pallas_call(
+        functools.partial(return_kernel, n),
+        out_shape=jax.ShapeDtypeStruct(block, parts.dtype),
+        in_specs=[pl.BlockSpec(memory_space=pl.ANY)],
+        out_specs=pl.BlockSpec(memory_space=pl.ANY),
+        scratch_shapes=[
+            pltpu.VMEM((2,) + block, parts.dtype),
+            pltpu.VMEM((2,) + block, parts.dtype),
+            pltpu.VMEM(block, parts.dtype),
+            pltpu.SemaphoreType.DMA((2,)),
+        ]
+        + [pltpu.SemaphoreType.DMA((n,))] * 8,
+        compiler_params=pltpu.CompilerParams(
+            collective_id=cid, has_side_effects=True, vmem_limit_bytes=VMEM_LIMIT
+        ),
+    )(parts)
 
 
 def skew(x, forward):
@@ -197,28 +386,27 @@
     cols = n_heads * DH
     cuts = n_dp // n_exp
     part = hidden // cuts
+    sizes = {"dp": n_dp, "tensor": n_t}
+    turn = lax.axis_index("tensor")
     SDS = jax.ShapeDtypeStruct
 
     packed = jnp.concatenate([w_query, w_key, w_value, w_out_t], axis=1)
     smalls = jnp.concatenate(
         [gain_attn[None], gain_moe[None], w_router.T, jnp.zeros((2, d_rows), BF)], axis=0
     )
-    experts_out = (
-        jnp.stack([w_gate, w_up, w_down_t])
-        .reshape(3, n_exp, d_rows, cuts, part)
-        .transpose(1, 3, 0, 2, 4)
-        .reshape(n_dp, 3, d_rows, part)
-    )
-    full, small_full, experts_in = exchange(
-        [packed, smalls, experts_out], (0, 0, 1), "dp", n_dp, 0
-    )
+    experts_out = [
+        jnp.stack([w[:, :, c * part : (c + 1) * part] for c in range(cuts)], axis=1).reshape(
+            n_dp, d_rows, part
+        )
+        for w in (w_gate, w_up, w_down_t)
+    ]
+    full, small_full = exchange(sizes, [packed, smalls], (0, 0), ("dp", "dp"), 0)
     full = full.reshape(width, 4 * cols)
     w_qkv, w_out = full[:, : 3 * cols], full[:, 3 * cols :]
     small_full = small_full.transpose(1, 0, 2).reshape(8, width)
     attn_gain_f = small_full[0].astype(F32)
     moe_gain_f = small_full[1].astype(F32)
     router_t = small_full[2 : 2 + n_exp]
-    e_gate, e_up, e_down = [experts_in[:, i].reshape(width, part) for i in range(3)]
 
     token_f = tokens.astype(F32)
     normed = rms_scale(token_f, attn_gain_f).astype(BF)
@@ -235,7 +423,10 @@
         dist_bias,
     )
     attn_part = mm(mixed, w_out, 1, 1).astype(BF)
-    (attn_parts,) = exchange([attn_part], (0,), "tensor", n_t, 1)
+    attn_parts, *experts_in = exchange(
+        sizes, [attn_part] + experts_out, (0, 1, 1, 1), ("tensor", "dp", "dp", "dp"), 1
+    )
+    e_gate, e_up, e_down = [w.reshape(width, part) for w in experts_in]
     residual = token_f + jnp.sum(attn_parts.astype(F32), axis=0)
     normed_moe = rms_scale(residual, moe_gain_f).astype(BF)
     logits = mm(normed_moe, router_t, 1, 1)
@@ -252,14 +443,16 @@
     pick = (place.T[:, None, :] == slot_ids[None, :, None]).astype(BF)
     gates = router * chosen.astype(F32)
     grad_final = cotangent.astype(F32)
-    d_rows_all = (gates.T[:, :, None] * grad_final[None]).astype(BF)
-    rows_all = jnp.concatenate(
-        [jnp.broadcast_to(normed_moe[None], (n_exp, seq, width)), d_rows_all], axis=2
-    )
+    quarter = width // 2
+    column = lax.rem(turn, 2) * quarter
+    is_out = turn < 2
+    grad_slice = lax.dynamic_slice_in_dim(grad_final, column, quarter, 1)
+    moe_slice = lax.dynamic_slice_in_dim(normed_moe, column, quarter, 1)
+    rows_all = jnp.where(is_out, moe_slice[None], (gates.T[:, :, None] * grad_slice[None]).astype(BF))
     sends = jnp.einsum("est,etd->esd", pick, rows_all, preferred_element_type=F32).astype(BF)
-    (arrived,) = exchange([sends], (cuts,), "dp", n_dp, 2)
-    arrived = arrived.reshape(n_dp * CAP, 2 * width)
-    rows_x, rows_d = arrived[:, :width], arrived[:, width:]
+    arrived = dispatch(sends, n_dp, cuts, 2).reshape(4, n_dp * CAP, quarter)
+    rows_x = jnp.concatenate([arrived[0], arrived[1]], axis=1)
+    rows_d = jnp.concatenate([arrived[2], arrived[3]], axis=1)
 
     gate_act = mm(rows_x, e_gate)
     up_act = mm(rows_x, e_up)
@@ -270,23 +463,31 @@
     d_gate_act, d_up_act = d_gate_act.astype(BF), d_up_act.astype(BF)
     part_out = mm(inner, e_down, 1, 1).astype(BF)
     part_dx = (mm(d_gate_act, e_gate, 1, 1) + mm(d_up_act, e_up, 1, 1)).astype(BF)
-    returns = jnp.concatenate([part_out, part_dx], axis=1).reshape(n_dp, CAP, 2 * width)
-    (returned,) = exchange([returns], (1,), "dp", n_dp, 3)
+    returns = jnp.stack(
+        [p[:, c : c + quarter] for p in (part_out, part_dx) for c in (0, quarter)]
+    ).reshape(4, n_dp, CAP, quarter)
+    returned = send_home(returns, n_dp, 3)
     g_down = mm(rows_d, inner, 0, 0).astype(BF)
     g_gate = mm(rows_x, d_gate_act, 0, 0).astype(BF)
     g_up = mm(rows_x, d_up_act, 0, 0).astype(BF)
 
-    returned = returned.reshape(n_exp, cuts * CAP, 2 * width)
+    returned = returned.reshape(n_exp, cuts * CAP, quarter)
     pick_back = jnp.tile(pick, (1, cuts, 1))
     home = jnp.einsum("est,esd->etd", pick_back, returned, preferred_element_type=F32)
-    moe_part = jnp.sum(gates.T[:, :, None] * home[:, :, :width], axis=0).astype(BF)
-    d_moe_part = jnp.sum(home[:, :, width:], axis=0).astype(BF)
-    d_router_part = jnp.sum(home[:, :, :width] * grad_final[None], axis=2)
-    moe_parts, d_moe_parts, d_router_parts = exchange(
-        [moe_part, d_moe_part, d_router_part], (0, 0, 0), "tensor", n_t, 4
-    )
-    moe_out = jnp.sum(moe_parts.astype(F32), axis=0)
-    d_moe = jnp.sum(d_moe_parts.astype(F32), axis=0)
+    scaled = jnp.where(is_out, gates.T, 1.0)
+    layer_part = jnp.sum(scaled[:, :, None] * home, axis=0).astype(BF)
+    d_router_part = jnp.where(is_out, jnp.sum(home * grad_slice[None], axis=2), 0.0)
+    g_exp = [g.reshape(n_dp, d_rows, part) for g in (g_gate, g_up, g_down)]
+    layer_parts, d_router_parts, *r_exp = exchange(
+        sizes,
+        [layer_part, d_router_part] + g_exp,
+        (0, 0, 1, 1, 1),
+        ("tensor", "tensor", "dp", "dp", "dp"),
+        4,
+    )
+    layer_parts = layer_parts.astype(F32)
+    moe_out = jnp.concatenate([layer_parts[0], layer_parts[1]], axis=1)
+    d_moe = jnp.concatenate([layer_parts[2], layer_parts[3]], axis=1)
     d_router = jnp.sum(d_router_parts, axis=0).T
     output = (residual + moe_out).astype(BF)
 
@@ -309,40 +510,40 @@
     )
     g_table = jnp.dot(d_dist, dist_hot, precision=HIGHEST)
     d_normed_part = mm(d_qkv, w_qkv, 1, 1).astype(BF)
-    (d_normed_parts,) = exchange([d_normed_part], (0,), "tensor", n_t, 5)
+    g_qkv = mm(normed, d_qkv, 0, 0)
+    g_attn = jnp.concatenate([g_qkv, g_out], axis=1).astype(BF).reshape(n_dp, d_rows, 4 * cols)
+    g_small = jnp.concatenate(
+        [g_moe_gain[None], g_router, jnp.zeros((7 - n_exp, width), F32)], axis=0
+    )
+    g_small = g_small.reshape(8, n_dp, d_rows).transpose(1, 0, 2)
+    d_normed_parts, r_attn, r_small, r_table = exchange(
+        sizes,
+        [d_normed_part, g_attn, g_small, g_table],
+        (0, 1, 1, 0),
+        ("tensor", "dp", "dp", "dp"),
+        5,
+    )
     d_normed = jnp.sum(d_normed_parts.astype(F32), axis=0)
-    g_qkv = mm(normed, d_qkv, 0, 0)
     unused, first_pull = jax.vjp(rms_scale, token_f, attn_gain_f)
     d_token_norm, g_attn_gain = first_pull(d_normed)
     grad_tokens = (d_residual + d_token_norm).astype(BF)
-
-    g_attn = jnp.concatenate([g_qkv, g_out], axis=1).astype(BF).reshape(n_dp, d_rows, 4 * cols)
-    g_small = jnp.concatenate(
-        [g_attn_gain[None], g_moe_gain[None], g_router, jnp.zeros((2, width), F32)], axis=0
-    )
-    g_small = g_small.reshape(8, n_dp, d_rows).transpose(1, 0, 2)
-    g_exp = jnp.stack([g.reshape(n_dp, d_rows, part) for g in (g_gate, g_up, g_down)], axis=1)
-    r_attn, r_small, r_exp, r_table = exchange(
-        [g_attn, g_small, g_exp, g_table], (1, 1, 1, 0), "dp", n_dp, 6
-    )
+    (r_gain,) = exchange(sizes, [g_attn_gain.reshape(n_dp, 1, d_rows)], (1,), ("dp",), 6)
     attn_total = jnp.sum(r_attn.astype(F32), axis=0)
     small_total = jnp.sum(r_small, axis=0)
-    exp_total = (
-        r_exp.reshape(n_exp, cuts, 3, d_rows, part)
-        .transpose(2, 0, 3, 1, 4)
-        .reshape(3, n_exp, d_rows, hidden)
-        .astype(F32)
-    )
+    exp_total = []
+    for r in r_exp:
+        r = r.reshape(n_exp, cuts, d_rows, part)
+        exp_total.append(jnp.concatenate([r[:, c] for c in range(cuts)], axis=2).astype(F32))
     return (
         output,
         grad_tokens,
-        small_total[0],
+        jnp.sum(r_gain, axis=0)[0],
         attn_total[:, :cols],
         attn_total[:, cols : 2 * cols],
         attn_total[:, 2 * cols : 3 * cols],
         attn_total[:, 3 * cols :],
-        small_total[1],
-        small_total[2 : 2 + n_exp].T,
+        small_total[0],
+        small_total[1 : 1 + n_exp].T,
         exp_total[0],
         exp_total[1],
         exp_total[2],

time: 486 us -> 303 us (0.62)
  Pallas kernels: 385 us -> 229 us
  local copies, waits for them, and re-layouts: 37.8 us -> 15.2 us
    pallas_call x7, Pallas kernels: 379 us -> 223 us  [the longest x5 154 us: exchange(): pl.pallas_call(functools.partial(exchange_kernel, sizes, kinds, axes), ou...]
    slice x5 -> x3, local copies, waits for them, and re-layouts: 11.7 us -> 2.74 us  [the longest x1 2.38 us: body(): rows_d = jnp.concatenate([arrived[2], arrived[3]], axis=1)]
    squeeze x4 -> x5, local copies, waits for them, and re-layouts: 9.77 us -> 1.68 us  [the longest x1 0.98 us: body(): d_moe = jnp.concatenate([layer_parts[2], layer_parts[3]], axis=1)]
    concatenate x6 -> x4, local copies, waits for them, and re-layouts: 6.08 us -> 0.25 us  [body(): jnp.concatenate([g_moe_gain[None], g_router, jnp.zeros((7 - n_exp, width)...]
where the time goes in v2:
time: 303 us; the launch traced here: 302 us
  Pallas kernels  229 us (76%)
  matrix products  32 us (11%)
  other arithmetic  24.6 us (8%)
  local copies, waits for them, and re-layouts  15.2 us (5%)
    pallas_call x5, Pallas kernels, exchange(): pl.pallas_call(functools.partial(exchange_kernel, sizes, kinds, axes), ou...  154 us
    pallas_call x1, Pallas kernels, dispatch(): pl.pallas_call(functools.partial(dispatch_kernel, n, cuts), out_shape=jax...  35.4 us
    pallas_call x1, Pallas kernels, send_home(): pl.pallas_call(functools.partial(return_kernel, n), out_shape=jax.ShapeDt...  34 us
    dot_general x19, matrix products, mm(): lax.dot_general(a, b, (((ca,), (cb,)), ((), ())), preferred_element_type=...  28.2 us

profile of v2, /device:TPU:0, one launch (start us, length us, event | category | flops | bytes accessed | tf_op | source)
XLA Modules:
  0.0 302.3 jit_solution(18271705142653958901)
XLA Ops:
  0.7 1.7 pad_maximum_fusion.9.refs_0_
  2.4 1.3 maximum_maximum_fusion.refs_1_
  3.8 33.2 %shard_map.255 = (bf16[8,96,768]{2,1,0:T(8,128)(2,1)}, bf16[8,8,96]{2,1,0:T(8,128)(2,1)}) custom-call(bf16[96,768]{1,0:T(8,128)(2,1)} %pad_maximum_fusion.9.refs_0_, bf16[8,96]{1,0:T(8,128)(2,1)} %maximum_maximum_fusion.refs_1_), custom_call_target="tpu_custom_call" | custom-call | tf_op jit(solution)/shard_map/pallas_call | solution.py:94
  39.1 1.9 convolution_convert_fusion.8.q_ref
  42.8 2.9 shard_map.256
  45.7 2.1 convolution_convert_fusion.7.refs_0_
  51.0 39.5 %shard_map.257 = (bf16[4,256,768]{2,1,0:T(8,128)(2,1)}, bf16[8,96,384]{2,1,0:T(8,128)(2,1)}, bf16[8,96,384]{2,1,0:T(8,128)(2,1)}, bf16[8,96,384]{2,1,0:T(8,128)(2,1)}) custom-call(bf16[256,768]{1,0:T(8,128)(2,1)} %convolution_convert_fusion.7.refs_0_, bf16[8,96,384]{2,1,0:T(8,128)(2,1)} %bitcast.132, bf16[8,96,384]{2,1,0:T(8,128)(2,1)} %bitcast.133, ...), custom_call_target="tpu_custom_call" | custom-call | tf_op jit(solution)/shard_map/pallas_call | solution.py:94
  90.6 1.7 convert_reduce_fusion.1
  95.6 1.2 convolution_convert_fusion.5.in_ref
  96.8 35.4 %shard_map.258 = bf16[4,8,144,384]{3,2,1,0:T(8,128)(2,1)} custom-call(bf16[4,144,384]{2,1,0:T(8,128)(2,1)} %convolution_convert_fusion.5.in_ref), custom_call_target="tpu_custom_call" | custom-call | tf_op jit(solution)/shard_map/pallas_call | solution.py:186
  132.2 2.4 fusion.52
  135.8 5.2 %multiply_convert_fusion.1 = (bf16[1152,384]{1,0:T(8,128)(2,1)S(1)}, f32[1152,384]{1,0:T(8,128)S(1)}, f32[1152,384]{1,0:T(8,128)S(1)}) fusion(f32[1152,384]{1,0:T(8,128)S(1)} %fusion.50, bf16[768,384]{1,0:T(8,128)(2,1)S(1)} %bitcast.148, bf16[1152,384]{1,0:T(8,128)(2,1)S(1)} %bitcast.141, bf16[1152,384]{1,0:T(8,128)(2,1)S(1)} %bitcast.145), kind=kOutput, calls=%fused_computation.13 | convolution fusion | flops 712212480 | bytes 8552448 | tf_op jit(solution)/shard_map/dot_general | solution.py:21
  141.0 1.8 multiply_convert_fusion
  147.1 34.0 %shard_map.259 = bf16[8,144,384]{2,1,0:T(8,128)(2,1)S(1)} custom-call(bf16[4,8,144,384]{3,2,1,0:T(8,128)(2,1)S(1)} %pad_maximum_fusion.in_ref), custom_call_target="tpu_custom_call" | custom-call | tf_op jit(solution)/shard_map/pallas_call | solution.py:272
  181.1 1.5 multiply_reduce_fusion
  183.2 2.0 convolution_convert_fusion.4
  185.2 2.0 convolution_convert_fusion.3
  187.2 2.0 convolution_convert_fusion.2
  189.2 41.6 %shard_map.260 = (bf16[4,256,384]{2,1,0:T(8,128)(2,1)}, f32[4,4,256]{2,1,0:T(4,128)}, bf16[8,96,384]{2,1,0:T(8,128)(2,1)}, bf16[8,96,384]{2,1,0:T(8,128)(2,1)}, bf16[8,96,384]{2,1,0:T(8,128)(2,1)}) custom-call(bf16[256,384]{1,0:T(8,128)(2,1)} %get-tuple-element.54.refs_0_, f32[4,256]{1,0:T(4,128)} %broadcast_select_fusion.1.refs_1_, ...), custom_call_target="tpu_custom_call" | custom-call | tf_op jit(solution)/shard_map/pallas_call | solution.py:94
  230.8 1.2 convert_element_type.152
  235.4 1.5 convolution_convert_fusion.10
  237.0 2.9 shard_map.261
  239.9 2.5 convolution_convert_fusion.6.refs_0_
  243.5 1.4 convolution_convert_fusion.1
  245.0 1.6 copy.83
  246.5 2.2 pad_maximum_fusion.3.refs_1_
  250.7 33.0 %shard_map.262 = (bf16[4,256,768]{2,1,0:T(8,128)(2,1)}, bf16[8,96,768]{2,1,0:T(8,128)(2,1)}, f32[8,8,96]{2,1,0:T(8,128)}, f32[8,3,32]{2,1,0:T(4,128)}) custom-call(bf16[256,768]{1,0:T(8,128)(2,1)} %convolution_convert_fusion.6.refs_0_, bf16[8,96,768]{2,1,0:T(8,128)(2,1)} %pad_maximum_fusion.3.refs_1_, f32[8,8,96]{2,1,0:T(8,128)} %maximum_bitcast_fusion.refs_2_, ...), custom_call_target="tpu_custom_call" | custom-call | tf_op jit(solution)/shard_map/pallas_call | solution.py:94
  283.8 1.7 convert_reduce_fusion
  287.5 6.7 %shard_map.263 = f32[8,1,96]{2,1,0:T(1,128)} custom-call(f32[8,1,96]{2,1,0:T(1,128)} %reshape.202.refs_0_), custom_call_target="tpu_custom_call" | custom-call | tf_op jit(solution)/shard_map/pallas_call | solution.py:94
  294.1 1.2 reduce_sum.170
  295.3 1.5 convert_reduce_fusion.2
  298.9 1.6 maximum_convert_fusion
  (131 shorter events, 28.5 us)
Async XLA Ops:
  0.6 42.0 %copy-start = (bf16[3,32]{1,0:T(4,128)(2,1)S(1)}, bf16[3,32]{1,0:T(4,128)(2,1)}, u32[]{:S(2)}) copy-start(bf16[3,32]{1,0:T(4,128)(2,1)} %param.31) | copy-start | bytes 580
  0.7 40.3 %copy-start.2 = (s32[1,256]{1,0:T(1,128)S(1)}, s32[1,256]{1,0:T(1,128)}, u32[]{:S(2)}) copy-start(s32[1,256]{1,0:T(1,128)} %seg_row_ref.1) | copy-start | bytes 3076
  0.7 40.5 %copy-start.24 = (s32[256]{0:T(256)S(1)}, s32[256]{0:T(256)}, u32[]{:S(2)}) copy-start(s32[256]{0:T(256)} %param.20) | copy-start | bytes 3076
  39.0 8.8 %copy-start.11 = (bf16[4,96,768]{2,1,0:T(8,128)(2,1)S(1)}, bf16[4,96,768]{2,1,0:T(8,128)(2,1)}, u32[]{:S(2)}) copy-start(bf16[4,96,768]{2,1,0:T(8,128)(2,1)} %param.28) | copy-start | bytes 1769476
  47.9 1.1 copy-start.12
  48.9 1.1 copy-start.13
  51.0 41.3 %copy-start.3 = (bf16[256,768]{1,0:T(8,128)(2,1)S(1)}, bf16[256,768]{1,0:T(8,128)(2,1)}, u32[]{:S(2)}) copy-start(bf16[256,768]{1,0:T(8,128)(2,1)} %param.16) | copy-start | bytes 1179652
  90.6 2.0 copy-start.21
  92.7 2.3 copy-start.23
  94.6 1.0 copy-start.17
  94.7 2.1 copy-start.4
  132.2 2.4 copy-start.10
  134.6 1.1 copy-start.9
  135.7 5.2 %copy-start.25 = (bf16[8,96,384]{2,1,0:T(8,128)(2,1)S(1)}, bf16[8,96,384]{2,1,0:T(8,128)(2,1)}, u32[]{:S(2)}) copy-start(bf16[8,96,384]{2,1,0:T(8,128)(2,1)} %get-tuple-element.38) | copy-start | bytes 1769476
  147.1 34.0 %copy-start.18 = (f32[256,384]{1,0:T(8,128)S(1)}, f32[256,384]{1,0:T(8,128)}, u32[]{:S(2)}) copy-start(f32[256,384]{1,0:T(8,128)} %constant_dynamic-slice_fusion) | copy-start | bytes 1179652
  232.1 1.0 copy-start.22
  233.1 1.0 copy-start.6
  233.1 1.1 copy-start.7
  233.1 1.2 copy-start.8
  245.0 3.8 %copy-start.5 = (bf16[256,768]{1,0:T(8,128)(2,1)S(1)}, bf16[256,768]{1,0:T(8,128)(2,1)}, u32[]{:S(2)}) copy-start(bf16[256,768]{1,0:T(8,128)(2,1)} %copy-done.4) | copy-start | bytes 1179652
  285.8 11.8 %copy-start.19 = (f32[8,8,96]{2,1,0:T(8,128)S(1)}, f32[8,8,96]{2,1,0:T(8,128)}, u32[]{:S(2)}) copy-start(f32[8,8,96]{2,1,0:T(8,128)} %get-tuple-element.46) | copy-start | bytes 73732
  285.8 12.9 %copy-start.16 = (bf16[8,96,384]{2,1,0:T(8,128)(2,1)S(1)}, bf16[8,96,384]{2,1,0:T(8,128)(2,1)}, u32[]{:S(2)}) copy-start(bf16[8,96,384]{2,1,0:T(8,128)(2,1)} %get-tuple-element.47) | copy-start | bytes 1769476
  286.8 12.0 %copy-start.15 = (bf16[8,96,384]{2,1,0:T(8,128)(2,1)S(1)}, bf16[8,96,384]{2,1,0:T(8,128)(2,1)}, u32[]{:S(2)}) copy-start(bf16[8,96,384]{2,1,0:T(8,128)(2,1)} %get-tuple-element.48) | copy-start | bytes 1769476
  298.9 1.6 copy-start.14
  298.9 3.4 %copy-start.1 = (bf16[3,32]{1,0:T(4,128)(2,1)S(1)}, bf16[3,32]{1,0:T(4,128)(2,1)}, u32[]{:S(2)}) copy-start(bf16[3,32]{1,0:T(4,128)(2,1)} %param.31) | copy-start | bytes 580
  300.5 1.2 copy-start.20

commit v3 on v2

--- a/solution.py
+++ b/solution.py
@@ -44,10 +44,67 @@
     lax.fori_loop(start, stop, one, 0)
 
 
-def exchange_kernel(sizes, kinds, axes, *refs):
+def fold_plan(n, in_ref, out_ref, held, came, load_sem, own_sem, *sems):
+    near, ring = sems[:2], sems[2:]
+    half = n // 2
+    me = lax.axis_index("dp")
+    low, high = lax.rem(me, 2), me // 2
+    other = 1 - low
+
+    def place(k):
+        return lax.rem(high + 1 + k, half)
+
+    def load(k):
+        s = place(k)
+        return pltpu.make_async_copy(in_ref.at[2 * s + low], held.at[s], load_sem.at[k])
+
+    def share(k):
+        s = place(k)
+        target = {"dp": 2 * high + other}
+        return push(in_ref.at[2 * s + other], came.at[s], near, k, target)
+
+    def send(k):
+        s = place(k)
+        return push(held.at[s], out_ref.at[high], ring, k, {"dp": 2 * s + low})
+
+    def begin(k):
+        load(k).start()
+        share(k).start()
+
+    def add(k):
+        s = place(k)
+        load(k).wait()
+        share(k).wait_recv()
+        held[s] = (held[s].astype(F32) + came[s].astype(F32)).astype(BF)
+
+    def step(k):
+        add(k)
+        send(k).start()
+
+    def start():
+        each(0, half, begin)
+
+    def run():
+        each(0, half - 1, step)
+        add(half - 1)
+        own = pltpu.make_async_copy(held.at[high], out_ref.at[high], own_sem)
+        own.start()
+        own.wait()
+
+    def finish():
+        each(0, half - 1, lambda k: send(k).wait())
+        each(0, half, lambda k: share(k).wait_send())
+
+    return start, run, finish
+
+
+def exchange_kernel(sizes, kinds, axes, fold, *refs):
     m = len(kinds)
-    ins, outs = refs[:m], refs[m : 2 * m]
-    local_sem, send_sem, recv_sem = refs[2 * m :]
+    f = m + fold
+    ins, outs = refs[:m], refs[f : f + m]
+    local_sem, send_sem, recv_sem = refs[2 * f : 2 * f + 3]
+    if fold:
+        plan = fold_plan(sizes["dp"], refs[m], refs[f + m], *refs[2 * f + 3 :])
     barrier = pltpu.get_barrier_semaphore()
     expected = 0
     for axis in sorted(set(axes)):
@@ -76,32 +133,49 @@
             device_id_type=MESH,
         )
 
+    if fold:
+        plan[0]()
     for a in range(m):
         each(1, sizes[axes[a]], lambda k, a=a: remote(a, k).start())
+    if fold:
+        plan[1]()
     for copy in locals_:
         copy.wait()
+    if fold:
+        plan[2]()
     for a in range(m):
         each(1, sizes[axes[a]], lambda k, a=a: remote(a, k).wait())
 
 
-def exchange(sizes, arrays, kinds, axes, cid):
+def exchange(sizes, arrays, kinds, axes, cid, fold=None):
     m = len(arrays)
     most = max(sizes[axis] for axis in axes)
     shapes = [
         jax.ShapeDtypeStruct((sizes[axis],) + (a.shape if k == 0 else a.shape[1:]), a.dtype)
         for a, k, axis in zip(arrays, kinds, axes)
     ]
+    scratch = [
+        pltpu.SemaphoreType.DMA((m,)),
+        pltpu.SemaphoreType.DMA((m, most)),
+        pltpu.SemaphoreType.DMA((m, most)),
+    ]
+    if fold is not None:
+        half = sizes["dp"] // 2
+        block = (half,) + fold.shape[1:]
+        arrays = arrays + [fold]
+        shapes = shapes + [jax.ShapeDtypeStruct(block, fold.dtype)]
+        scratch = scratch + [pltpu.VMEM(block, fold.dtype)] * 2
+        scratch = scratch + [pltpu.SemaphoreType.DMA((half,)), pltpu.SemaphoreType.DMA]
+        scratch = scratch + [pltpu.SemaphoreType.DMA((half,))] * 4
     return pl.pallas_call(
-        functools.partial(exchange_kernel, sizes, kinds, axes),
+        functools.partial(exchange_kernel, sizes, kinds, axes, int(fold is not None)),
         out_shape=shapes,
-        in_specs=[pl.BlockSpec(memory_space=pl.ANY)] * m,
-        out_specs=[pl.BlockSpec(memory_space=pl.ANY)] * m,
-        scratch_shapes=[
-            pltpu.SemaphoreType.DMA((m,)),
-            pltpu.SemaphoreType.DMA((m, most)),
-            pltpu.SemaphoreType.DMA((m, most)),
-        ],
-        compiler_params=pltpu.CompilerParams(collective_id=cid, has_side_effects=True),
+        in_specs=[pl.BlockSpec(memory_space=pl.ANY)] * len(arrays),
+        out_specs=[pl.BlockSpec(memory_space=pl.ANY)] * len(arrays),
+        scratch_shapes=scratch,
+        compiler_params=pltpu.CompilerParams(
+            collective_id=cid, has_side_effects=True, vmem_limit_bytes=VMEM_LIMIT
+        ),
     )(*arrays)
 
 
@@ -124,6 +198,67 @@
         device_id=device,
         device_id_type=MESH,
     )
+
+
+def gather_kernel(n, m, *refs):
+    ins, outs = refs[:m], refs[m : 2 * m]
+    local_sem = refs[2 * m]
+    ring, near = refs[2 * m + 1 : 2 * m + 3], refs[2 * m + 3 :]
+    me = lax.axis_index("dp")
+    partner = me + 1 - 2 * lax.rem(me, 2)
+    barrier = pltpu.get_barrier_semaphore()
+    expected = greet(barrier, "dp", n)
+    locals_ = [
+        pltpu.make_async_copy(ins[a], outs[a].at[me], local_sem.at[a]) for a in range(m)
+    ]
+    for copy in locals_:
+        copy.start()
+    pl.semaphore_wait(barrier, expected)
+
+    def first(a, k):
+        target = lax.rem(me + 2 * k, n)
+        return push(ins[a], outs[a].at[me], ring, (a, k), {"dp": target})
+
+    def own(a):
+        return push(ins[a], outs[a].at[me], near, (a, 0), {"dp": partner})
+
+    def forward(a, k):
+        here = outs[a].at[lax.rem(me - 2 * k + n, n)]
+        return push(here, here, near, (a, k), {"dp": partner})
+
+    for a in range(m):
+        each(1, n // 2, lambda k, a=a: first(a, k).start())
+        own(a).start()
+
+    def step(a, k):
+        first(a, k).wait_recv()
+        forward(a, k).start()
+
+    for a in range(m):
+        each(1, n // 2, lambda k, a=a: step(a, k))
+    for copy in locals_:
+        copy.wait()
+    for a in range(m):
+        own(a).wait()
+
+        def finish(k, a=a):
+            first(a, k).wait_send()
+            forward(a, k).wait()
+
+        each(1, n // 2, finish)
+
+
+def gather(arrays, n, cid):
+    m = len(arrays)
+    return pl.pallas_call(
+        functools.partial(gather_kernel, n, m),
+        out_shape=[jax.ShapeDtypeStruct((n,) + a.shape, a.dtype) for a in arrays],
+        in_specs=[pl.BlockSpec(memory_space=pl.ANY)] * m,
+        out_specs=[pl.BlockSpec(memory_space=pl.ANY)] * m,
+        scratch_shapes=[pltpu.SemaphoreType.DMA((m,))]
+        + [pltpu.SemaphoreType.DMA((m, n // 2))] * 4,
+        compiler_params=pltpu.CompilerParams(collective_id=cid, has_side_effects=True),
+    )(*arrays)
 
 
 def dispatch_kernel(n, cuts, in_ref, out_ref, local_sem, *sems):
@@ -400,7 +535,7 @@
         )
         for w in (w_gate, w_up, w_down_t)
     ]
-    full, small_full = exchange(sizes, [packed, smalls], (0, 0), ("dp", "dp"), 0)
+    full, small_full = gather([packed, smalls], n_dp, 0)
     full = full.reshape(width, 4 * cols)
     w_qkv, w_out = full[:, : 3 * cols], full[:, 3 * cols :]
     small_full = small_full.transpose(1, 0, 2).reshape(8, width)
@@ -516,12 +651,13 @@
         [g_moe_gain[None], g_router, jnp.zeros((7 - n_exp, width), F32)], axis=0
     )
     g_small = g_small.reshape(8, n_dp, d_rows).transpose(1, 0, 2)
-    d_normed_parts, r_attn, r_small, r_table = exchange(
+    d_normed_parts, r_small, r_table, r_attn = exchange(
         sizes,
-        [d_normed_part, g_attn, g_small, g_table],
-        (0, 1, 1, 0),
-        ("tensor", "dp", "dp", "dp"),
+        [d_normed_part, g_small, g_table],
+        (0, 1, 0),
+        ("tensor", "dp", "dp"),
         5,
+        g_attn,
     )
     d_normed = jnp.sum(d_normed_parts.astype(F32), axis=0)
     unused, first_pull = jax.vjp(rms_scale, token_f, attn_gain_f)

time: 303 us -> 281 us (0.927)
  Pallas kernels: 229 us -> 213 us
  other arithmetic: 24.6 us -> 18.2 us
    pallas_call x5, Pallas kernels: 154 us -> 139 us  [the longest x4 114 us: exchange(): pl.pallas_call(functools.partial(exchange_kernel, sizes, kinds, axes, int...]
where the time goes in v3:
time: 281 us; the launch traced here: 280 us
  Pallas kernels  213 us (76%)
  matrix products  30.2 us (11%)
  other arithmetic  18.2 us (6%)
  local copies, waits for them, and re-layouts  17.4 us (6%)
    pallas_call x4, Pallas kernels, exchange(): pl.pallas_call(functools.partial(exchange_kernel, sizes, kinds, axes, int...  114 us
    pallas_call x1, Pallas kernels, dispatch(): pl.pallas_call(functools.partial(dispatch_kernel, n, cuts), out_shape=jax...  34.4 us
    pallas_call x1, Pallas kernels, send_home(): pl.pallas_call(functools.partial(return_kernel, n), out_shape=jax.ShapeDt...  33.3 us
    dot_general x19, matrix products, mm(): lax.dot_general(a, b, (((ca,), (cb,)), ((), ())), preferred_element_type=...  27.6 us
    pallas_call x1, Pallas kernels, gather(): pl.pallas_call(functools.partial(gather_kernel, n, m), out_shape=[jax.Sha...  25.3 us
    pallas_call x2, Pallas kernels, local_call(): pl.pallas_call(kernel, out_shape=out_shape, compiler_params=pltpu.Compile...  5.78 us

profile of v3, /device:TPU:0, one launch (start us, length us, event | category | flops | bytes accessed | tf_op | source)
XLA Modules:
  0.0 280.1 jit_solution(2504720568437648397)
XLA Ops:
  0.7 1.7 pad_maximum_fusion.9.refs_0_
  2.4 1.3 maximum_maximum_fusion.refs_1_
  3.8 25.3 %shard_map.255 = (bf16[8,96,768]{2,1,0:T(8,128)(2,1)}, bf16[8,8,96]{2,1,0:T(8,128)(2,1)}) custom-call(bf16[96,768]{1,0:T(8,128)(2,1)} %pad_maximum_fusion.9.refs_0_, bf16[8,96]{1,0:T(8,128)(2,1)} %maximum_maximum_fusion.refs_1_), custom_call_target="tpu_custom_call" | custom-call | tf_op jit(solution)/shard_map/pallas_call | solution.py:253
  30.0 1.2 fusion.19
  31.1 1.9 convolution_convert_fusion.8.q_ref
  34.9 2.9 %shard_map.256 = (bf16[256,192]{1,0:T(8,128)(2,1)S(1)}, f32[3,256,256]{2,1,0:T(8,128)S(1)}) custom-call(bf16[256,576]{1,0:T(8,128)(2,1)S(1)} %convolution_convert_fusion.8.q_ref, s32[1,256]{1,0:T(1,128)S(1)} %copy-done.2, s32[256,1]{1,0:T(8,128)S(1)} %copy.77.seg_col_ref, f32[3,256]{1,0:T(4,128)S(1)} %convolution_bitcast_fusion.dist_ref), custom_call_target="tpu_custom_call" | custom-call | tf_op jit(solution)/shard_map/pallas_call | solution.py:478
  37.8 1.4 convolution_convert_fusion.7.refs_0_
  41.6 41.5 %shard_map.257 = (bf16[4,256,768]{2,1,0:T(8,128)(2,1)S(1)}, bf16[8,96,384]{2,1,0:T(8,128)(2,1)S(1)}, bf16[8,96,384]{2,1,0:T(8,128)(2,1)S(1)}, bf16[8,96,384]{2,1,0:T(8,128)(2,1)S(1)}) custom-call(bf16[256,768]{1,0:T(8,128)(2,1)S(1)} %convolution_convert_fusion.7.refs_0_, bf16[8,96,384]{2,1,0:T(8,128)(2,1)S(1)} %bitcast.125, ...), custom_call_target="tpu_custom_call" | custom-call | tf_op jit(solution)/shard_map/pallas_call | solution.py:170
  86.5 1.3 multiply_convert_fusion.3
  89.3 1.2 convolution_convert_fusion.5.in_ref
  90.6 34.4 %shard_map.258 = bf16[4,8,144,384]{3,2,1,0:T(8,128)(2,1)} custom-call(bf16[4,144,384]{2,1,0:T(8,128)(2,1)} %convolution_convert_fusion.5.in_ref), custom_call_target="tpu_custom_call" | custom-call | tf_op jit(solution)/shard_map/pallas_call | solution.py:321
  125.0 2.3 fusion.52
  128.4 5.2 %multiply_convert_fusion.1 = (bf16[1152,384]{1,0:T(8,128)(2,1)S(1)}, f32[1152,384]{1,0:T(8,128)S(1)}, f32[1152,384]{1,0:T(8,128)S(1)}) fusion(f32[1152,384]{1,0:T(8,128)S(1)} %fusion.50, bf16[768,384]{1,0:T(8,128)(2,1)S(1)} %bitcast.129, bf16[1152,384]{1,0:T(8,128)(2,1)S(1)} %bitcast.153, bf16[1152,384]{1,0:T(8,128)(2,1)S(1)} %bitcast.157), kind=kOutput, calls=%fused_computation.12 | convolution fusion | flops 712212480 | bytes 8552448 | tf_op jit(solution)/shard_map/dot_general | solution.py:21
  133.6 1.8 multiply_convert_fusion
  136.6 1.1 fusion
  139.8 33.3 %shard_map.259 = bf16[8,144,384]{2,1,0:T(8,128)(2,1)S(1)} custom-call(bf16[4,8,144,384]{3,2,1,0:T(8,128)(2,1)S(1)} %pad_maximum_fusion.in_ref), custom_call_target="tpu_custom_call" | custom-call | tf_op jit(solution)/shard_map/pallas_call | solution.py:407
  174.3 1.2 convolution_convert_fusion.4
  175.5 1.2 convolution_convert_fusion.3
  176.7 1.2 convolution_convert_fusion.2
  177.9 41.2 %shard_map.260 = (bf16[4,256,384]{2,1,0:T(8,128)(2,1)S(1)}, f32[4,4,256]{2,1,0:T(4,128)S(1)}, bf16[8,96,384]{2,1,0:T(8,128)(2,1)S(1)}, bf16[8,96,384]{2,1,0:T(8,128)(2,1)S(1)}, bf16[8,96,384]{2,1,0:T(8,128)(2,1)S(1)}) custom-call(bf16[256,384]{1,0:T(8,128)(2,1)S(1)} %get-tuple-element.54.refs_0_, f32[4,256]{1,0:T(4,128)S(1)} %broadcast_select_fusion.1.refs_1_, ...), custom_call_target="tpu_custom_call" | custom-call | tf_op jit(solution)/shard_map/pallas_call | solution.py:170
  220.4 1.9 multiply_reduce_fusion.2
  224.2 1.5 convolution_convert_fusion.10
  225.9 2.9 %shard_map.261 = (bf16[256,576]{1,0:T(8,128)(2,1)S(1)}, f32[3,256]{1,0:T(4,128)S(1)}) custom-call(bf16[256,576]{1,0:T(8,128)(2,1)S(1)} %convolution_convert_fusion.8.q_ref, f32[3,256,256]{2,1,0:T(8,128)S(1)} %get-tuple-element.41.prob_ref, bf16[256,192]{1,0:T(8,128)(2,1)S(1)} %copy.82.dmix_ref), custom_call_target="tpu_custom_call" | custom-call | tf_op jit(solution)/shard_map/pallas_call | solution.py:478
  228.8 1.8 convolution_convert_fusion.6.refs_0_
  231.3 2.2 convolution_convert_fusion.9
  233.4 1.9 copy.85
  235.3 1.4 convolution_convert_fusion.1
  236.7 2.3 copy.84
  239.0 1.4 pad_maximum_fusion.3.refs_3_
  240.4 24.2 %shard_map.262 = (bf16[4,256,768]{2,1,0:T(8,128)(2,1)S(1)}, f32[8,8,96]{2,1,0:T(8,128)S(1)}, f32[8,3,32]{2,1,0:T(4,128)S(1)}, bf16[4,96,768]{2,1,0:T(8,128)(2,1)S(1)}) custom-call(bf16[256,768]{1,0:T(8,128)(2,1)S(1)} %convolution_convert_fusion.6.refs_0_, f32[8,8,96]{2,1,0:T(8,128)S(1)} %maximum_bitcast_fusion.refs_1_, f32[3,32]{1,0:T(4,128)S(1)} %fusion.34.refs_2_, ...), custom_call_target="tpu_custom_call" | custom-call | tf_op jit(solution)/shard_map/pallas_call | solution.py:170
  266.9 7.1 %shard_map.263 = f32[8,1,96]{2,1,0:T(1,128)S(1)} custom-call(f32[8,1,96]{2,1,0:T(1,128)S(1)} %reshape.202.refs_0_), custom_call_target="tpu_custom_call" | custom-call | tf_op jit(solution)/shard_map/pallas_call | solution.py:170
  276.7 1.6 maximum_convert_fusion
  (131 shorter events, 25.9 us)
Async XLA Ops:
  0.6 34.0 %copy-start = (bf16[3,32]{1,0:T(4,128)(2,1)S(1)}, bf16[3,32]{1,0:T(4,128)(2,1)}, u32[]{:S(2)}) copy-start(bf16[3,32]{1,0:T(4,128)(2,1)} %param.31) | copy-start | bytes 580
  0.7 32.4 %copy-start.2 = (s32[1,256]{1,0:T(1,128)S(1)}, s32[1,256]{1,0:T(1,128)}, u32[]{:S(2)}) copy-start(s32[1,256]{1,0:T(1,128)} %seg_row_ref.1) | copy-start | bytes 3076
  0.7 32.5 %copy-start.23 = (s32[256]{0:T(256)S(1)}, s32[256]{0:T(256)}, u32[]{:S(2)}) copy-start(s32[256]{0:T(256)} %param.20) | copy-start | bytes 3076
  31.1 8.1 %copy-start.17 = (bf16[4,96,768]{2,1,0:T(8,128)(2,1)S(1)}, bf16[4,96,768]{2,1,0:T(8,128)(2,1)}, u32[]{:S(2)}) copy-start(bf16[4,96,768]{2,1,0:T(8,128)(2,1)} %param.28) | copy-start | bytes 1769476
  39.2 1.1 copy-start.18
  40.3 1.1 copy-start.19
  41.6 41.8 %copy-start.6 = (bf16[256,768]{1,0:T(8,128)(2,1)S(1)}, bf16[256,768]{1,0:T(8,128)(2,1)}, u32[]{:S(2)}) copy-start(bf16[256,768]{1,0:T(8,128)(2,1)} %param.16) | copy-start | bytes 1179652
  83.1 1.3 copy-start.21
  83.1 1.4 copy-start.12
  84.6 3.5 %copy-start.22 = (s32[256,2]{0,1:T(2,128)S(1)}, s32[256,2]{0,1:T(2,128)}, u32[]{:S(2)}) copy-start(s32[256,2]{0,1:T(2,128)} %param.19) | copy-start | bytes 6148
  87.8 1.5 copy-start.9
  133.6 4.3 %copy-start.24 = (bf16[1152,384]{1,0:T(8,128)(2,1)}, bf16[1152,384]{1,0:T(8,128)(2,1)S(1)}, u32[]{:S(2)}) copy-start(bf16[1152,384]{1,0:T(8,128)(2,1)S(1)} %get-tuple-element.61) | copy-start | bytes 2654212
  135.4 1.1 copy-start.15
  139.8 33.3 %copy-start.20 = (bf16[4,2,144,256]{3,2,1,0:T(8,128)(2,1)S(1)}, bf16[4,2,144,256]{3,2,1,0:T(8,128)(2,1)}, u32[]{:S(2)}) copy-start(bf16[4,2,144,256]{3,2,1,0:T(8,128)(2,1)} %tile.4) | copy-start | bytes 1769476
  173.1 1.2 copy-start.16
  175.4 1.2 copy-start.25
  220.3 2.0 copy-start.3
  220.3 2.0 copy-start.11
  220.3 2.0 copy-start.13
  223.4 0.9 copy-start.4
  225.9 4.7 %copy-start.10 = (bf16[256,768]{1,0:T(8,128)(2,1)S(1)}, bf16[256,768]{1,0:T(8,128)(2,1)}, u32[]{:S(2)}) copy-start(bf16[256,768]{1,0:T(8,128)(2,1)} %copy-done.9) | copy-start | bytes 1179652
  228.8 6.6 %copy-start.7 = (bf16[256,768]{1,0:T(8,128)(2,1)S(1)}, bf16[256,768]{1,0:T(8,128)(2,1)}, u32[]{:S(2)}) copy-start(bf16[256,768]{1,0:T(8,128)(2,1)} %param.16) | copy-start | bytes 1179652
  236.7 2.3 copy-start.14
  240.4 24.5 %copy-start.8 = (bf16[256,768]{1,0:T(8,128)(2,1)S(1)}, bf16[256,768]{1,0:T(8,128)(2,1)}, u32[]{:S(2)}) copy-start(bf16[256,768]{1,0:T(8,128)(2,1)} %param.16) | copy-start | bytes 1179652
  264.7 1.1 copy-start.5
  276.7 3.4 %copy-start.1 = (bf16[3,32]{1,0:T(4,128)(2,1)S(1)}, bf16[3,32]{1,0:T(4,128)(2,1)}, u32[]{:S(2)}) copy-start(bf16[3,32]{1,0:T(4,128)(2,1)} %param.31) | copy-start | bytes 580
